TPU v7x, 32 devices: a whole 2x2x4 slice. The times are simulated.
32 devices in a mesh: dp: 8 (over z, x), fsdp: 4 (over y, core).
Axes of the slice: x: 2, y: 2, z: 4, core: 2. Of those that a mesh axis runs over, the one named last changes fastest.
Arguments:
- tokens: bfloat16 [32, 2048, 512], P(('dp', 'fsdp')), may hold values from -6 to 6
- cotangent: bfloat16 [32, 2048, 512], P(('dp', 'fsdp')), may hold values from -6 to 6
- known_genes: int32 [32, 2048], P(('dp', 'fsdp')), may hold values 0 or 1
- cell_kind: int32 [32], P(('dp', 'fsdp')), may hold values from 0 to 1, as said below
- gene_counts: int32 [32, 4], P(('dp', 'fsdp')), may hold values from 0 to 2048, as said below
- study_index: int32 [32, 4], P(('dp', 'fsdp')), may hold values from 0 to 7, as said below
- qkv_weight: float32 [512, 1536], P('fsdp'), may hold values from -0.25 to 0.25
- qkv_first: float32 [512, 1536], P('fsdp'), may hold values from -1536 to 1536
- qkv_second: float32 [512, 1536], P('fsdp'), may hold values from 65536 to 262144
- proj_weight: float32 [512, 512], P('fsdp'), may hold values from -6 to 6
- proj_first: float32 [512, 512], P('fsdp'), may hold values from -128 to 128
- proj_second: float32 [512, 512], P('fsdp'), may hold values from 512 to 2048
- up_weight: float32 [512, 512], P('fsdp'), may hold values from -0.25 to 0.25
- up_first: float32 [512, 512], P('fsdp'), may hold values from -1536 to 1536
- up_second: float32 [512, 512], P('fsdp'), may hold values from 65536 to 262144
- down_weight: float32 [512, 512], P('fsdp'), may hold values from -0.25 to 0.25
- down_first: float32 [512, 512], P('fsdp'), may hold values from -768 to 768
- down_second: float32 [512, 512], P('fsdp'), may hold values from 16384 to 65536
- norm_params: float32 [4, 512], P(None, 'fsdp'), may hold values from -0.5 to 1.4, as said below
- norm_first: float32 [4, 512], P(None, 'fsdp'), may hold values from -1536 to 1536
- norm_second: float32 [4, 512], P(None, 'fsdp'), may hold values from 65536 to 262144
Outputs:
- out: bfloat16 [32, 2048, 512], P(('dp', 'fsdp'))
- input_grad: bfloat16 [32, 2048, 512], P(('dp', 'fsdp'))
- study_mean: float32 [8, 512], replicated
- study_var: float32 [8, 512], replicated
- qkv_first_new: float32 [512, 1536], P('fsdp')
- qkv_second_new: float32 [512, 1536], P('fsdp')
- qkv_weight_new: float32 [512, 1536], P('fsdp')
- qkv_weight_copy: bfloat16 [512, 1536], P('fsdp')
- proj_first_new: float32 [512, 512], P('fsdp')
- proj_second_new: float32 [512, 512], P('fsdp')
- proj_weight_new: float32 [512, 512], P('fsdp')
- proj_weight_copy: bfloat16 [512, 512], P('fsdp')
- up_first_new: float32 [512, 512], P('fsdp')
- up_second_new: float32 [512, 512], P('fsdp')
- up_weight_new: float32 [512, 512], P('fsdp')
- up_weight_copy: bfloat16 [512, 512], P('fsdp')
- down_first_new: float32 [512, 512], P('fsdp')
- down_second_new: float32 [512, 512], P('fsdp')
- down_weight_new: float32 [512, 512], P('fsdp')
- down_weight_copy: bfloat16 [512, 512], P('fsdp')
- norm_first_new: float32 [4, 512], P(None, 'fsdp')
- norm_second_new: float32 [4, 512], P(None, 'fsdp')
- norm_params_new: float32 [4, 512], P(None, 'fsdp')
- norm_params_copy: bfloat16 [4, 512], P(None, 'fsdp')
- matrix_norms: float32 [3, 4], replicated
Inputs may be any that keep to these rules, and one draw needn't show every extreme that they name: `cell_kind`: both kinds occur in every draw. `gene_counts`: slots 1 and up of a group with cell_kind 1 hold 0. A long cell has 1024 genes or more, some long cell exactly 2048; a short cell has 256 or more, some short cell exactly 512. `study_index`: every study has a used cell slot. `norm_params`: rows 0 and 2 are gains, rows 1 and 3 biases.
All inputs are finite; a program needn't handle non-finite values. No bound on the sum of `known_genes` on one device may be relied on, other than what follows from the above.
Results may differ from a plain program's by a relative error of at most 0.019.
Values may be sent and summed in bfloat16 or wider, within the bound.
No kernel may reach another device: no remote copies, remote signals or barrier semaphores. Data moves between devices by JAX's collectives and lax.ppermute only.
A program may use at most 256 MiB of HBM per device.

v0:
```python
from functools import partial

import jax
import jax.numpy as jnp
from jax import lax
from jax.sharding import PartitionSpec as P

HEADS = 8
HDIM = 64
SHORT_LENGTH = 512
STUDY_COUNT = 8
STEP = 5


BETA = 0.5
ADAM_EPS = 1e-06
NORM_EPS = 1e-05
MATRIX_RATE = 0.5
VECTOR_RATE = 0.3
MATRIX_DECAY = 0.01
MASKED = -1000000000.0


def layer_norm(inputs, gain_vec, bias_vec):
    row_mean = jnp.mean(inputs, axis=-1, keepdims=True)
    centred = inputs - row_mean
    variance = jnp.mean(centred * centred, axis=-1, keepdims=True)
    return centred * lax.rsqrt(variance + NORM_EPS) * gain_vec + bias_vec


def cell_layout(kind_flag, gene_count, known_flag):
    position = jnp.arange(known_flag.shape[0], dtype=jnp.int32)
    segment = position // SHORT_LENGTH
    cell_ids = jnp.where(kind_flag == 1, 0, segment)
    cell_start = jnp.where(kind_flag == 1, 0, segment * SHORT_LENGTH)
    slot_index = jnp.arange(gene_count.shape[0], dtype=jnp.int32)
    cell_limit = jnp.sum(
        jnp.where(cell_ids[:, None] == slot_index[None, :], gene_count[None, :], 0), axis=1
    )
    key_ok = (position - cell_start < cell_limit) & ((known_flag == 1) | (position == cell_start))
    return (cell_ids, key_ok)


def masked_scores(queries, keys, cell_ids, key_ok, begin_row, block_rows):
    position = jnp.arange(keys.shape[0], dtype=jnp.int32)
    row_ids = begin_row + jnp.arange(block_rows, dtype=jnp.int32)
    query_block = lax.dynamic_slice_in_dim(queries, begin_row, block_rows, 0)
    cell_block = lax.dynamic_slice_in_dim(cell_ids, begin_row, block_rows, 0)
    scores = jnp.einsum(
        "bhd,khd->hbk", query_block, keys, preferred_element_type=jnp.float32
    ) * keys.shape[2] ** (-0.5)
    allowed = (cell_block[:, None] == cell_ids[None, :]) & (
        key_ok[None, :] | (row_ids[:, None] == position[None, :])
    )
    return (jnp.where(allowed[None], scores, MASKED), query_block)


def attend_forward(group_item):
    queries, keys, values, cell_ids, key_ok = group_item
    length = keys.shape[0]
    block_rows = min(512, length)
    begins = jnp.arange(length // block_rows, dtype=jnp.int32) * block_rows

    def one_block(begin_row):
        scores, query_block = masked_scores(queries, keys, cell_ids, key_ok, begin_row, block_rows)
        row_top = jnp.max(scores, axis=-1, keepdims=True)
        raised = jnp.exp(scores - row_top)
        row_total = jnp.sum(raised, axis=-1, keepdims=True)
        attn_probs = (raised / row_total).astype(jnp.bfloat16)
        context = jnp.einsum("hbk,khd->bhd", attn_probs, values, preferred_element_type=jnp.float32)
        return (context, (row_top + jnp.log(row_total))[..., 0])

    context, log_total = lax.map(one_block, begins)
    return (context.reshape(length, -1), log_total)


def attend_backward(group_item):
    queries, keys, values, cell_ids, key_ok, log_total, grad_context = group_item
    length = keys.shape[0]
    block_rows = min(512, length)
    begins = jnp.arange(length // block_rows, dtype=jnp.int32) * block_rows
    score_scale = keys.shape[2] ** (-0.5)

    def one_block(running, block_item):
        grad_keys, grad_values = running
        begin_row, block_total = block_item
        scores, query_block = masked_scores(queries, keys, cell_ids, key_ok, begin_row, block_rows)
        attn_probs = jnp.exp(scores - block_total[..., None])
        grad_block = lax.dynamic_slice_in_dim(grad_context, begin_row, block_rows, 0)
        grad_probs = jnp.einsum(
            "bhd,khd->hbk", grad_block, values, preferred_element_type=jnp.float32
        )
        row_inner = jnp.sum(attn_probs * grad_probs, axis=-1, keepdims=True)
        grad_scores = (attn_probs * (grad_probs - row_inner)).astype(jnp.bfloat16)
        grad_queries = (
            jnp.einsum("hbk,khd->bhd", grad_scores, keys, preferred_element_type=jnp.float32)
            * score_scale
        )
        grad_keys = (
            grad_keys
            + jnp.einsum(
                "hbk,bhd->khd", grad_scores, query_block, preferred_element_type=jnp.float32
            )
            * score_scale
        )
        grad_values = grad_values + jnp.einsum(
            "hbk,bhd->khd",
            attn_probs.astype(jnp.bfloat16),
            grad_block,
            preferred_element_type=jnp.float32,
        )
        return ((grad_keys, grad_values), grad_queries)

    zero_grads = jnp.zeros(keys.shape, jnp.float32)
    (grad_keys, grad_values), grad_queries = lax.scan(
        one_block, (zero_grads, zero_grads), (begins, log_total)
    )
    return jnp.stack([grad_queries.reshape(keys.shape), grad_keys, grad_values], axis=1)


def adam_terms(gradient, first_old, second_old):
    first_new = BETA * first_old + (1.0 - BETA) * gradient
    second_new = BETA * second_old + (1.0 - BETA) * gradient * gradient
    debias = 1.0 - BETA**STEP
    update = first_new / debias / (jnp.sqrt(second_new / debias) + ADAM_EPS)
    return (first_new, second_new, update)


def shards(
    tokens,
    cotangent,
    known_genes,
    cell_kind,
    gene_counts,
    study_index,
    qkv_weight,
    qkv_first,
    qkv_second,
    proj_weight,
    proj_first,
    proj_second,
    up_weight,
    up_first,
    up_second,
    down_weight,
    down_first,
    down_second,
    norm_params,
    norm_first,
    norm_second,
):
    masters = (qkv_weight, proj_weight, up_weight, down_weight, norm_params)
    firsts_old = (qkv_first, proj_first, up_first, down_first, norm_first)
    seconds_old = (qkv_second, proj_second, up_second, down_second, norm_second)
    copies = tuple((weight.astype(jnp.bfloat16) for weight in masters))
    gathered = (
        lax.all_gather(copies[0], "fsdp", axis=0, tiled=True),
        lax.all_gather(copies[1], "fsdp", axis=0, tiled=True),
        lax.all_gather(copies[2], "fsdp", axis=0, tiled=True),
        lax.all_gather(copies[3], "fsdp", axis=0, tiled=True),
        lax.all_gather(copies[4], "fsdp", axis=1, tiled=True),
    )
    f_qkv, f_proj, f_up, f_down, f_norm = gathered
    forward_norms = f_norm.astype(jnp.float32)
    groups, length, feat_width = tokens.shape
    row_count = groups * length
    cell_ids, key_ok = jax.vmap(cell_layout)(cell_kind, gene_counts, known_genes)
    tokens_flat = tokens.reshape(row_count, feat_width)
    qkv = jnp.dot(tokens_flat, f_qkv, preferred_element_type=jnp.float32).astype(jnp.bfloat16)
    split_qkv = qkv.reshape(groups, length, 3, HEADS, HDIM)
    queries = split_qkv[:, :, 0]
    keys = split_qkv[:, :, 1]
    values = split_qkv[:, :, 2]
    context, log_total = lax.map(attend_forward, (queries, keys, values, cell_ids, key_ok))
    context_low = context.reshape(row_count, feat_width).astype(jnp.bfloat16)
    first_sum = tokens_flat.astype(jnp.float32) + jnp.dot(
        context_low, f_proj, preferred_element_type=jnp.float32
    )
    middle = layer_norm(first_sum, forward_norms[0], forward_norms[1])
    middle_low = middle.astype(jnp.bfloat16)
    hidden = jnp.dot(middle_low, f_up, preferred_element_type=jnp.float32)
    active, pull_active = jax.vjp(partial(jax.nn.gelu, approximate=False), hidden)
    active_low = active.astype(jnp.bfloat16)
    second_sum = middle + jnp.dot(active_low, f_down, preferred_element_type=jnp.float32)
    result = layer_norm(second_sum, forward_norms[2], forward_norms[3])
    out_low = result.astype(jnp.bfloat16)
    first_cells = out_low.reshape(groups, -1, SHORT_LENGTH, feat_width)[:, :, 0, :].astype(
        jnp.float32
    )
    slot_index = jnp.arange(first_cells.shape[1], dtype=jnp.int32)
    used_slots = (cell_kind[:, None] == 0) | (slot_index[None, :] == 0)
    member_cell = (
        (study_index[:, :, None] == jnp.arange(STUDY_COUNT, dtype=jnp.int32)[None, None, :])
        & used_slots[:, :, None]
    ).astype(jnp.float32)
    local_counts = jnp.sum(member_cell, axis=(0, 1))
    local_sums = jnp.sum(member_cell[:, :, :, None] * first_cells[:, :, None, :], axis=(0, 1))
    local_squares = jnp.sum(
        member_cell[:, :, :, None] * (first_cells * first_cells)[:, :, None, :], axis=(0, 1)
    )
    study_counts, study_sums, study_squares = lax.psum(
        (local_counts, local_sums, local_squares), ("dp", "fsdp")
    )
    study_mean = study_sums / study_counts[:, None]
    study_var = study_squares / study_counts[:, None] - study_mean * study_mean
    again = (
        lax.all_gather(copies[0], "fsdp", axis=0, tiled=True),
        lax.all_gather(copies[1], "fsdp", axis=0, tiled=True),
        lax.all_gather(copies[2], "fsdp", axis=0, tiled=True),
        lax.all_gather(copies[3], "fsdp", axis=0, tiled=True),
        lax.all_gather(copies[4], "fsdp", axis=1, tiled=True),
    )
    b_qkv, b_proj, b_up, b_down, b_norm = again
    back_norms = b_norm.astype(jnp.float32)
    _, pull_second = jax.vjp(layer_norm, second_sum, back_norms[2], back_norms[3])
    grad_second, grad_gain2, grad_bias2 = pull_second(
        cotangent.reshape(row_count, feat_width).astype(jnp.float32)
    )
    grad_branch = grad_second.astype(jnp.bfloat16)
    grad_down = jnp.einsum("rf,rd->fd", active_low, grad_branch, preferred_element_type=jnp.float32)
    grad_active = jnp.dot(grad_branch, b_down.T, preferred_element_type=jnp.float32)
    (grad_hidden,) = pull_active(grad_active)
    hidden_grad_low = grad_hidden.astype(jnp.bfloat16)
    grad_up = jnp.einsum(
        "rd,rf->df", middle_low, hidden_grad_low, preferred_element_type=jnp.float32
    )
    grad_middle = grad_second + jnp.dot(hidden_grad_low, b_up.T, preferred_element_type=jnp.float32)
    _, pull_first = jax.vjp(layer_norm, first_sum, back_norms[0], back_norms[1])
    grad_first, grad_gain1, grad_bias1 = pull_first(grad_middle)
    proj_grad_low = grad_first.astype(jnp.bfloat16)
    grad_proj = jnp.einsum(
        "rc,rd->cd", context_low, proj_grad_low, preferred_element_type=jnp.float32
    )
    grad_context = jnp.dot(proj_grad_low, b_proj.T, preferred_element_type=jnp.float32).astype(
        jnp.bfloat16
    )
    grad_context = grad_context.reshape(groups, length, HEADS, HDIM)
    grad_qkv = lax.map(
        attend_backward, (queries, keys, values, cell_ids, key_ok, log_total, grad_context)
    )
    qkv_grad_low = grad_qkv.reshape(row_count, 3 * feat_width).astype(jnp.bfloat16)
    grad_qkv_weight = jnp.einsum(
        "rd,rk->dk", tokens_flat, qkv_grad_low, preferred_element_type=jnp.float32
    )
    grad_tokens = grad_first + jnp.dot(qkv_grad_low, b_qkv.T, preferred_element_type=jnp.float32)
    input_grad = grad_tokens.astype(jnp.bfloat16).reshape(tokens.shape)
    grad_norm = jnp.stack([grad_gain1, grad_bias1, grad_gain2, grad_bias2])
    local_grads = (grad_qkv_weight, grad_proj, grad_up, grad_down, grad_norm)
    pieces = (
        lax.psum_scatter(
            local_grads[0].astype(jnp.bfloat16), "fsdp", scatter_dimension=0, tiled=True
        ).astype(jnp.float32),
        lax.psum_scatter(
            local_grads[1].astype(jnp.bfloat16), "fsdp", scatter_dimension=0, tiled=True
        ).astype(jnp.float32),
        lax.psum_scatter(
            local_grads[2].astype(jnp.bfloat16), "fsdp", scatter_dimension=0, tiled=True
        ).astype(jnp.float32),
        lax.psum_scatter(
            local_grads[3].astype(jnp.bfloat16), "fsdp", scatter_dimension=0, tiled=True
        ).astype(jnp.float32),
        lax.psum_scatter(
            local_grads[4].astype(jnp.bfloat16), "fsdp", scatter_dimension=1, tiled=True
        ).astype(jnp.float32),
    )
    shares = (
        lax.psum(pieces[0].astype(jnp.bfloat16), "dp").astype(jnp.float32),
        lax.psum(pieces[1].astype(jnp.bfloat16), "dp").astype(jnp.float32),
        lax.psum(pieces[2].astype(jnp.bfloat16), "dp").astype(jnp.float32),
        lax.psum(pieces[3].astype(jnp.bfloat16), "dp").astype(jnp.float32),
        lax.psum(pieces[4].astype(jnp.bfloat16), "dp").astype(jnp.float32),
    )
    moved = [adam_terms(shares[index], firsts_old[index], seconds_old[index]) for index in range(5)]
    updates = [moved[index][2] + MATRIX_DECAY * masters[index] for index in range(4)]
    square_terms = [jnp.sum(masters[index] * masters[index]) for index in range(4)]
    square_terms = square_terms + [jnp.sum(updates[index] * updates[index]) for index in range(4)]
    total_squares = lax.psum(jnp.stack(square_terms), "fsdp")
    weight_norms = jnp.sqrt(total_squares[:4])
    update_norms = jnp.sqrt(total_squares[4:])
    trust = weight_norms / update_norms
    results = []
    for index in range(5):
        if index < 4:
            new_weight = masters[index] - MATRIX_RATE * trust[index] * updates[index]
        else:
            new_weight = masters[index] - VECTOR_RATE * moved[index][2]
        results.extend(
            [moved[index][0], moved[index][1], new_weight, new_weight.astype(jnp.bfloat16)]
        )
    matrix_norms = jnp.stack([weight_norms, update_norms, trust])
    return (
        out_low.reshape(tokens.shape),
        input_grad,
        study_mean,
        study_var,
        results[0],
        results[1],
        results[2],
        results[3],
        results[4],
        results[5],
        results[6],
        results[7],
        results[8],
        results[9],
        results[10],
        results[11],
        results[12],
        results[13],
        results[14],
        results[15],
        results[16],
        results[17],
        results[18],
        results[19],
        matrix_norms,
    )


def solution(mesh):
    return jax.shard_map(
        shards,
        mesh=mesh,
        in_specs=(
            P(("dp", "fsdp"), None, None),
            P(("dp", "fsdp"), None, None),
            P(("dp", "fsdp"), None),
            P(("dp", "fsdp")),
            P(("dp", "fsdp"), None),
            P(("dp", "fsdp"), None),
            P("fsdp", None),
            P("fsdp", None),
            P("fsdp", None),
            P("fsdp", None),
            P("fsdp", None),
            P("fsdp", None),
            P("fsdp", None),
            P("fsdp", None),
            P("fsdp", None),
            P("fsdp", None),
            P("fsdp", None),
            P("fsdp", None),
            P(None, "fsdp"),
            P(None, "fsdp"),
            P(None, "fsdp"),
        ),
        out_specs=(
            P(("dp", "fsdp"), None, None),
            P(("dp", "fsdp"), None, None),
            P(),
            P(),
            P("fsdp", None),
            P("fsdp", None),
            P("fsdp", None),
            P("fsdp", None),
            P("fsdp", None),
            P("fsdp", None),
            P("fsdp", None),
            P("fsdp", None),
            P("fsdp", None),
            P("fsdp", None),
            P("fsdp", None),
            P("fsdp", None),
            P("fsdp", None),
            P("fsdp", None),
            P("fsdp", None),
            P("fsdp", None),
            P(None, "fsdp"),
            P(None, "fsdp"),
            P(None, "fsdp"),
            P(None, "fsdp"),
            P(),
        ),
        check_vma=False,
    )
```

profile of v0, /device:TPU:0, one launch (start us, length us, event | category | flops | bytes accessed | tf_op | source)
XLA Modules:
  0.0 1104.2 jit_solution(6188076631522577055)
XLA Ops:
  57.5 202.7 %while.45 = (s32[]{:T(128)}, bf16[4,512,8,64]{1,3,2,0:T(8,128)(2,1)}, f32[4,8,512]{2,1,0:T(8,128)S(1)}, s32[4]{0:T(128)S(1)}, s32[2048]{0:T(1024)S(1)}, /*index=...) while((s32[]{:T(128)}, ...), condition=%wide.region_4.5_spmd, body=%wide.region_1.4_spmd.sunk | while | flops 2252337664 | bytes 110776504 | solution.py:73
  300.9 535.4 %while.46 = (s32[]{:T(128)}, f32[2048,8,64]{0,2,1:T(8,128)}, f32[2048,8,64]{0,2,1:T(8,128)}, bf16[4,512,8,64]{1,0,3,2:T(4,128)(2,1)}, s32[4]{0:T(128)S(1)}, /*in...) while((s32[]{:T(128)}, f32[2048,8,64]{0,2,1:T(8,128)}, ...), condition=%wide.region_15.16_spmd.clone, body=%wide.region_13.15_spmd.clone.sunk | while | flops 5454164480 | bytes 350851360 | solution.py:115
  317.4 17.5 %fusion.139 = f32[8,512,2048]{2,1,0:T(8,128)} fusion(bf16[2048,8,64]{0,2,1:T(8,128)(2,1)} %get-tuple-element.669, bf16[2048,8,64]{0,2,1:T(8,128)(2,1)} %get-tuple-element.668, s32[]{:T(128)S(6)} %select_n.124), kind=kOutput, calls=%fused_computation.31.clone.1 | convolution fusion | flops 1073741824 | bytes 36175876 | tf_op jit(solution)/shard_map/while/body/eval_jaxpr/while/body/eval_jaxpr/bhd,khd->hbk/dot_general | solution.py:90
  335.0 26.3 %multiply_reduce_fusion.16 = (f32[8,512]{1,0:T(8,128)S(1)}, f32[8,512,2048]{2,1,0:T(8,128)}) fusion(f32[8,512,2048]{2,1,0:T(8,128)} %fusion.139, f32[8,512]{1,0:T(8,128)S(1)} %dynamic-slice_bitcast_fusion.2, bf16[2048,8,64]{0,2,1:T(8,128)(2,1)S(1)} %get-tuple-element.666, bf16[2048,8,64]{0,2,1:T(8,128)(2,1)} %get-tuple-element.663, ...), kind=kOutput, calls=%fused_computation.19.clone.1 | convolution fusion | flops 1115680768 | bytes 70811648 | tf_op jit(solution)/shard_map/while/body/eval_jaxpr/while/body/eval_jaxpr/bhd,khd->hbk/dot_general | solution.py:49
  361.2 27.4 %multiply_convert_fusion.3 = bf16[8,512,2048]{2,1,0:T(8,128)(2,1)} fusion(f32[8,512,2048]{2,1,0:T(8,128)} %get-tuple-element.590, f32[8,512,2048]{2,1,0:T(8,128)} %fusion.139, f32[8,512]{1,0:T(8,128)S(1)} %get-tuple-element.591), kind=kLoop, calls=%fused_computation.18.clone.1 | loop fusion | flops 25165824 | bytes 83902464 | tf_op jit(solution)/shard_map/while/body/eval_jaxpr/while/body/eval_jaxpr/convert_element_type | solution.py:94
  422.4 19.3 %dynamic_update_slice.28 = bf16[4,512,8,64]{1,0,3,2:T(4,128)(2,1)} dynamic-update-slice(bf16[4,512,8,64]{1,0,3,2:T(4,128)(2,1)} %get-tuple-element.646, bf16[1,512,8,64]{1,0,3,2:T(2,128)(2,1)S(1)} %copy.118, s32[]{:T(128)S(6)} %copy.135, s32[]{:T(128)} %constant.104.clone.1..sunk.1, s32[]{:T(128)} %constant.104.clone.1..sunk.1, s32[]{:T(128)} %constant.104.clone.1..sunk.1) | dynamic-update-slice | bytes 1048580 | tf_op jit(solution)/shard_map/while/body/eval_jaxpr/while/body/jit(dynamic_update_index_in_dim)/dynamic_update_slice | solution.py:73
  446.5 17.5 %fusion.139 = f32[8,512,2048]{2,1,0:T(8,128)} fusion(bf16[2048,8,64]{0,2,1:T(8,128)(2,1)} %get-tuple-element.669, bf16[2048,8,64]{0,2,1:T(8,128)(2,1)} %get-tuple-element.668, s32[]{:T(128)S(6)} %select_n.124), kind=kOutput, calls=%fused_computation.31.clone.1 | convolution fusion | flops 1073741824 | bytes 36175876 | tf_op jit(solution)/shard_map/while/body/eval_jaxpr/while/body/eval_jaxpr/bhd,khd->hbk/dot_general | solution.py:90
  464.0 26.3 %multiply_reduce_fusion.16 = (f32[8,512]{1,0:T(8,128)S(1)}, f32[8,512,2048]{2,1,0:T(8,128)}) fusion(f32[8,512,2048]{2,1,0:T(8,128)} %fusion.139, f32[8,512]{1,0:T(8,128)S(1)} %dynamic-slice_bitcast_fusion.2, bf16[2048,8,64]{0,2,1:T(8,128)(2,1)S(1)} %get-tuple-element.666, bf16[2048,8,64]{0,2,1:T(8,128)(2,1)} %get-tuple-element.663, ...), kind=kOutput, calls=%fused_computation.19.clone.1 | convolution fusion | flops 1115680768 | bytes 70811648 | tf_op jit(solution)/shard_map/while/body/eval_jaxpr/while/body/eval_jaxpr/bhd,khd->hbk/dot_general | solution.py:49
  490.2 27.4 %multiply_convert_fusion.3 = bf16[8,512,2048]{2,1,0:T(8,128)(2,1)} fusion(f32[8,512,2048]{2,1,0:T(8,128)} %get-tuple-element.590, f32[8,512,2048]{2,1,0:T(8,128)} %fusion.139, f32[8,512]{1,0:T(8,128)S(1)} %get-tuple-element.591), kind=kLoop, calls=%fused_computation.18.clone.1 | loop fusion | flops 25165824 | bytes 83902464 | tf_op jit(solution)/shard_map/while/body/eval_jaxpr/while/body/eval_jaxpr/convert_element_type | solution.py:94
  553.9 19.3 %dynamic_update_slice.28 = bf16[4,512,8,64]{1,0,3,2:T(4,128)(2,1)} dynamic-update-slice(bf16[4,512,8,64]{1,0,3,2:T(4,128)(2,1)} %get-tuple-element.646, bf16[1,512,8,64]{1,0,3,2:T(2,128)(2,1)S(1)} %copy.118, s32[]{:T(128)S(6)} %copy.135, s32[]{:T(128)} %constant.104.clone.1..sunk.1, s32[]{:T(128)} %constant.104.clone.1..sunk.1, s32[]{:T(128)} %constant.104.clone.1..sunk.1) | dynamic-update-slice | bytes 1048580 | tf_op jit(solution)/shard_map/while/body/eval_jaxpr/while/body/jit(dynamic_update_index_in_dim)/dynamic_update_slice | solution.py:73
  578.0 17.5 %fusion.139 = f32[8,512,2048]{2,1,0:T(8,128)} fusion(bf16[2048,8,64]{0,2,1:T(8,128)(2,1)} %get-tuple-element.669, bf16[2048,8,64]{0,2,1:T(8,128)(2,1)} %get-tuple-element.668, s32[]{:T(128)S(6)} %select_n.124), kind=kOutput, calls=%fused_computation.31.clone.1 | convolution fusion | flops 1073741824 | bytes 36175876 | tf_op jit(solution)/shard_map/while/body/eval_jaxpr/while/body/eval_jaxpr/bhd,khd->hbk/dot_general | solution.py:90
  595.5 26.3 %multiply_reduce_fusion.16 = (f32[8,512]{1,0:T(8,128)S(1)}, f32[8,512,2048]{2,1,0:T(8,128)}) fusion(f32[8,512,2048]{2,1,0:T(8,128)} %fusion.139, f32[8,512]{1,0:T(8,128)S(1)} %dynamic-slice_bitcast_fusion.2, bf16[2048,8,64]{0,2,1:T(8,128)(2,1)S(1)} %get-tuple-element.666, bf16[2048,8,64]{0,2,1:T(8,128)(2,1)} %get-tuple-element.663, ...), kind=kOutput, calls=%fused_computation.19.clone.1 | convolution fusion | flops 1115680768 | bytes 70811648 | tf_op jit(solution)/shard_map/while/body/eval_jaxpr/while/body/eval_jaxpr/bhd,khd->hbk/dot_general | solution.py:49
  621.7 27.4 %multiply_convert_fusion.3 = bf16[8,512,2048]{2,1,0:T(8,128)(2,1)} fusion(f32[8,512,2048]{2,1,0:T(8,128)} %get-tuple-element.590, f32[8,512,2048]{2,1,0:T(8,128)} %fusion.139, f32[8,512]{1,0:T(8,128)S(1)} %get-tuple-element.591), kind=kLoop, calls=%fused_computation.18.clone.1 | loop fusion | flops 25165824 | bytes 83902464 | tf_op jit(solution)/shard_map/while/body/eval_jaxpr/while/body/eval_jaxpr/convert_element_type | solution.py:94
  685.4 19.3 %dynamic_update_slice.28 = bf16[4,512,8,64]{1,0,3,2:T(4,128)(2,1)} dynamic-update-slice(bf16[4,512,8,64]{1,0,3,2:T(4,128)(2,1)} %get-tuple-element.646, bf16[1,512,8,64]{1,0,3,2:T(2,128)(2,1)S(1)} %copy.118, s32[]{:T(128)S(6)} %copy.135, s32[]{:T(128)} %constant.104.clone.1..sunk.1, s32[]{:T(128)} %constant.104.clone.1..sunk.1, s32[]{:T(128)} %constant.104.clone.1..sunk.1) | dynamic-update-slice | bytes 1048580 | tf_op jit(solution)/shard_map/while/body/eval_jaxpr/while/body/jit(dynamic_update_index_in_dim)/dynamic_update_slice | solution.py:73
  709.5 17.5 %fusion.139 = f32[8,512,2048]{2,1,0:T(8,128)} fusion(bf16[2048,8,64]{0,2,1:T(8,128)(2,1)} %get-tuple-element.669, bf16[2048,8,64]{0,2,1:T(8,128)(2,1)} %get-tuple-element.668, s32[]{:T(128)S(6)} %select_n.124), kind=kOutput, calls=%fused_computation.31.clone.1 | convolution fusion | flops 1073741824 | bytes 36175876 | tf_op jit(solution)/shard_map/while/body/eval_jaxpr/while/body/eval_jaxpr/bhd,khd->hbk/dot_general | solution.py:90
  727.0 26.2 %multiply_reduce_fusion.16 = (f32[8,512]{1,0:T(8,128)S(1)}, f32[8,512,2048]{2,1,0:T(8,128)}) fusion(f32[8,512,2048]{2,1,0:T(8,128)} %fusion.139, f32[8,512]{1,0:T(8,128)S(1)} %dynamic-slice_bitcast_fusion.2, bf16[2048,8,64]{0,2,1:T(8,128)(2,1)S(1)} %get-tuple-element.666, bf16[2048,8,64]{0,2,1:T(8,128)(2,1)} %get-tuple-element.663, ...), kind=kOutput, calls=%fused_computation.19.clone.1 | convolution fusion | flops 1115680768 | bytes 70811648 | tf_op jit(solution)/shard_map/while/body/eval_jaxpr/while/body/eval_jaxpr/bhd,khd->hbk/dot_general | solution.py:49
  753.2 27.4 %multiply_convert_fusion.3 = bf16[8,512,2048]{2,1,0:T(8,128)(2,1)} fusion(f32[8,512,2048]{2,1,0:T(8,128)} %get-tuple-element.590, f32[8,512,2048]{2,1,0:T(8,128)} %fusion.139, f32[8,512]{1,0:T(8,128)S(1)} %get-tuple-element.591), kind=kLoop, calls=%fused_computation.18.clone.1 | loop fusion | flops 25165824 | bytes 83902464 | tf_op jit(solution)/shard_map/while/body/eval_jaxpr/while/body/eval_jaxpr/convert_element_type | solution.py:94
  816.8 19.3 %dynamic_update_slice.28 = bf16[4,512,8,64]{1,0,3,2:T(4,128)(2,1)} dynamic-update-slice(bf16[4,512,8,64]{1,0,3,2:T(4,128)(2,1)} %get-tuple-element.646, bf16[1,512,8,64]{1,0,3,2:T(2,128)(2,1)S(1)} %copy.118, s32[]{:T(128)S(6)} %copy.135, s32[]{:T(128)} %constant.104.clone.1..sunk.1, s32[]{:T(128)} %constant.104.clone.1..sunk.1, s32[]{:T(128)} %constant.104.clone.1..sunk.1) | dynamic-update-slice | bytes 1048580 | tf_op jit(solution)/shard_map/while/body/eval_jaxpr/while/body/jit(dynamic_update_index_in_dim)/dynamic_update_slice | solution.py:73
  890.8 19.4 %reduce-scatter.10.cloned.1.call-done = bf16[128,512]{1,0:T(8,128)(2,1)} async-done(((bf16[512,512]{1,0:T(8,128)(2,1)}), bf16[128,512]{1,0:T(8,128)(2,1)}) %reduce-scatter.10.cloned.1.call-update) | async-done | bytes 131088 | tf_op jit(solution)/shard_map/reduce_scatter | solution.py:253
  910.2 24.0 %reduce-scatter.14.cloned.1.call-done = bf16[128,512]{1,0:T(8,128)(2,1)} async-done(((bf16[512,512]{1,0:T(8,128)(2,1)}), bf16[128,512]{1,0:T(8,128)(2,1)}) %reduce-scatter.14.cloned.1.call-update) | async-done | bytes 131088 | tf_op jit(solution)/shard_map/reduce_scatter | solution.py:259
  934.3 24.2 %reduce-scatter.12.cloned.1.call-done = bf16[128,512]{1,0:T(8,128)(2,1)} async-done(((bf16[512,512]{1,0:T(8,128)(2,1)}), bf16[128,512]{1,0:T(8,128)(2,1)}) %reduce-scatter.12.cloned.1.call-update) | async-done | bytes 131088 | tf_op jit(solution)/shard_map/reduce_scatter | solution.py:256
  958.6 40.0 %all-reduce = (f32[8,512]{1,0:T(8,128)S(1)}, f32[8]{0:T(128)S(1)}, f32[8,512]{1,0:T(8,128)S(1)}) all-reduce(f32[8,512]{1,0:T(8,128)S(1)} %get-tuple-element.344, f32[8]{0:T(128)S(1)} %convert_reduce_fusion, f32[8,512]{1,0:T(8,128)S(1)} %get-tuple-element.343), channel_id=1, replica_groups=mesh['dp'=8,'fsdp'=4] {'dp','fsdp'}, use_global_device_ids=true, to_apply=%region_17.18 | all-reduce | flops 8200 | bytes 65600 | tf_op jit(solution)/shard_map/psum | solution.py:201
  1000.1 21.1 %psum.71 = bf16[4,128]{1,0:T(4,128)(2,1)S(1)} all-reduce(bf16[4,128]{1,0:T(4,128)(2,1)S(1)} %copy.87), channel_id=1, replica_groups=mesh['dp'=8,'fsdp'=4] {'dp'}, use_global_device_ids=true, to_apply=%region_44.45 | all-reduce | flops 512 | bytes 2048 | tf_op jit(solution)/shard_map/psum | solution.py:271
  1021.8 39.2 %all-reduce.4.cloned.1.call-done = (bf16[128,1536]{0,1:T(8,128)(2,1)}, bf16[128,512]{1,0:T(8,128)(2,1)}, bf16[128,512]{1,0:T(8,128)(2,1)}, bf16[128,512]{1,0:T(8,128)(2,1)}) async-done(((bf16[128,1536]{0,1:T(8,128)(2,1)}, bf16[128,512]{1,0:T(8,128)(2,1)}, bf16[128,512]{1,0:T(8,128)(2,1)}, bf16[128,512]{1,0:T(8,128)(2,1)}), (bf16[128,1536]{0,1:T(8,128)(2,1)}, bf16[128,512]{1,0:T(8,128)(2,1)}, ...) | async-done | bytes 786448 | tf_op jit(solution)/shard_map/psum | solution.py:267
  (259 shorter events, 528.0 us)
Async XLA Ops:
  7.2 42.3 %copy-start.10 = (bf16[1,2048,512]{2,1,0:T(8,128)(2,1)S(1)}, bf16[1,2048,512]{2,1,0:T(8,128)(2,1)}, u32[]{:S(2)}) copy-start(bf16[1,2048,512]{2,1,0:T(8,128)(2,1)} %param.25) | copy-start | bytes 6291460
  7.2 42.3 %all-gather.2.cloned.1.call-start = ((), (), s32[]{:S(2)}) async-start(), calls=%async_computation.5 | async-start | bytes 1966080 | tf_op jit(solution)/shard_map/all_gather | solution.py:157
  10.3 878.6 %reduce-scatter.16.cloned.1.call-start = ((), (), s32[]{:S(2)}) async-start(), calls=%async_computation.9 | async-start | bytes 1966080
  267.7 10.5 copy-start.7
  267.7 11.9 %copy-start.18 = (bf16[512,512]{1,0:T(8,128)(2,1)S(1)}, bf16[512,512]{1,0:T(8,128)(2,1)}, u32[]{:S(2)}) copy-start(bf16[512,512]{1,0:T(8,128)(2,1)} %all_gather.24) | copy-start | bytes 1572868
  404.4 10.7 copy-start
  534.6 10.7 copy-start
  545.4 7.7 copy-start.4
  666.2 10.7 copy-start
  676.9 7.7 copy-start.4
  797.6 10.7 copy-start
  808.3 7.6 copy-start.4
  855.7 54.6 %reduce-scatter.10.cloned.1.call-start = ((), (), s32[]{:S(2)}) async-start(), calls=%async_computation.6 | async-start | bytes 655360 | tf_op jit(solution)/shard_map/reduce_scatter | solution.py:253
  860.1 74.2 %reduce-scatter.14.cloned.1.call-start = ((), (), s32[]{:S(2)}) async-start(), calls=%async_computation.8 | async-start | bytes 655360 | tf_op jit(solution)/shard_map/reduce_scatter | solution.py:259
  865.3 93.1 %reduce-scatter.12.cloned.1.call-start = ((), (), s32[]{:S(2)}) async-start(), calls=%async_computation.7 | async-start | bytes 655360 | tf_op jit(solution)/shard_map/reduce_scatter | solution.py:256
  869.9 129.4 %reduce-scatter.18.cloned.1.call-start = ((), (), s32[]{:S(2)}) async-start(), calls=%async_computation.10 | async-start | bytes 163840
  878.2 143.0 %copy-start.27 = (f32[4,128]{1,0:T(4,128)S(1)}, f32[4,128]{1,0:T(4,128)}, u32[]{:S(2)}) copy-start(f32[4,128]{1,0:T(4,128)} %param.43) | copy-start | bytes 6148
  878.2 143.0 %copy-start.33 = (f32[4,128]{1,0:T(4,128)S(1)}, f32[4,128]{1,0:T(4,128)}, u32[]{:S(2)}) copy-start(f32[4,128]{1,0:T(4,128)} %param.45) | copy-start | bytes 6148
  878.2 143.0 %copy-start.34 = (f32[4,128]{1,0:T(4,128)S(1)}, f32[4,128]{1,0:T(4,128)}, u32[]{:S(2)}) copy-start(f32[4,128]{1,0:T(4,128)} %param.44) | copy-start | bytes 6148
  878.2 182.8 %all-reduce.4.cloned.1.call-start = ((), (), s32[]{:S(2)}) async-start(), calls=%async_computation.11 | async-start | bytes 1572864 | tf_op jit(solution)/shard_map/psum | solution.py:267
  888.1 176.8 %copy-start.15 = (f32[128,512]{1,0:T(8,128)S(1)}, f32[128,512]{1,0:T(8,128)}, u32[]{:S(2)}) copy-start(f32[128,512]{1,0:T(8,128)} %param.34) | copy-start | bytes 786436
  888.1 176.8 %copy-start.19 = (f32[128,512]{1,0:T(8,128)S(1)}, f32[128,512]{1,0:T(8,128)}, u32[]{:S(2)}) copy-start(f32[128,512]{1,0:T(8,128)} %param.35) | copy-start | bytes 786436
  958.4 109.1 %copy-start.13 = (f32[128,512]{1,0:T(8,128)S(1)}, f32[128,512]{1,0:T(8,128)}, u32[]{:S(2)}) copy-start(f32[128,512]{1,0:T(8,128)} %param.40) | copy-start | bytes 786436
  958.4 109.1 %copy-start.14 = (f32[128,512]{1,0:T(8,128)S(1)}, f32[128,512]{1,0:T(8,128)}, u32[]{:S(2)}) copy-start(f32[128,512]{1,0:T(8,128)} %param.37) | copy-start | bytes 786436
  (26 other events, 93.4 us)
Sparse Core Ops, SparseCore 0:
  10.4 25.1 all-gather.1
  855.8 29.5 reduce-scatter.15
  888.6 21.6 reduce-scatter.9
  912.6 21.6 reduce-scatter.13
  936.7 21.6 reduce-scatter.11
  961.3 19.5 reduce-scatter.17
  985.6 75.3 all-reduce.3
where the time goes:
time: 1120 us; the launch traced here: 1100 us
  matrix products  491 us (44%)
  other arithmetic  229 us (20%)
  local copies, waits for them, and re-layouts  131 us (12%)
  waiting for transfers between devices  107 us (10%)
  blocking collectives  99.5 us (9%)
  loops' own time  28.1 us (3%)
  between operations  18.4 us (2%)
    dot_general x8, matrix products, masked_scores(): jnp.einsum('bhd,khd->hbk', query_block, keys, preferred_element_type=jnp....  166 us
    convert_element_type x4, other arithmetic, one_block(): grad_scores = (attn_probs * (grad_probs - row_inner)).astype(jnp.bfloat16)  110 us
    dynamic_update_slice x8, local copies, waits for them, and re-layouts, attend_forward(): context, log_total = lax.map(one_block, begins)  80.7 us
    dot_general x4, matrix products, one_block(): jnp.einsum('bhd,khd->hbk', grad_block, values, preferred_element_type=jnp...  70.1 us
    dot_general x4, matrix products, one_block(): jnp.einsum('hbk,bhd->khd', attn_probs.astype(jnp.bfloat16), grad_block, p...  66.9 us
    dot_general x4, matrix products, one_block(): jnp.einsum('hbk,khd->bhd', attn_probs, values, preferred_element_type=jnp...  62.2 us
    reduce_sum x4, other arithmetic, one_block(): row_total = jnp.sum(raised, axis=-1, keepdims=True)  59.9 us
    psum x1, blocking collectives, shards(): lax.psum((local_counts, local_sums, local_squares), ('dp', 'fsdp'))  40 us
  transfers between devices with their start and end apart: 7, of which 4 were waited for; matrix products, arithmetic and copies ran while one was open for 4% of the time, Pallas kernels for 0%

commit v1 on v0

v1 whole, which is shorter than its diff:
```python
from functools import partial

import jax
import jax.numpy as jnp
from jax import lax
from jax.experimental import pallas as pl
from jax.experimental.pallas import tpu as pltpu
from jax.sharding import PartitionSpec as P

HEADS = 8
HDIM = 64
SHORT_LENGTH = 512
STUDY_COUNT = 8
STEP = 5
PAIR = 2 * HDIM
PAIRS = HEADS // 2
KEY_BLOCK = 256
TAIL = 128


BETA = 0.5
ADAM_EPS = 1e-06
NORM_EPS = 1e-05
MATRIX_RATE = 0.5
VECTOR_RATE = 0.3
MATRIX_DECAY = 0.01
MASKED = -1000000000.0
SAFE_SCORE = 40.0

BF = jnp.bfloat16
F32 = jnp.float32
NN = (((1,), (0,)), ((), ()))
NT = (((1,), (1,)), ((), ()))
TN = (((0,), (0,)), ((), ()))
SMEM = pl.BlockSpec(memory_space=pltpu.SMEM)
ANY = pl.BlockSpec(memory_space=pl.ANY)
VMEM_LIMIT = 60 * 2**20


def mm(left, right, dims):
    return lax.dot_general(left, right, dims, preferred_element_type=F32)


def whole(*shape):
    return pl.BlockSpec(shape, lambda *_: (0,) * len(shape))


def params():
    return pltpu.CompilerParams(vmem_limit_bytes=VMEM_LIMIT)


def cost(flops, nbytes, trans=0):
    return pl.CostEstimate(flops=int(flops), bytes_accessed=int(nbytes), transcendentals=int(trans))


def iota(shape, dim):
    return lax.broadcasted_iota(jnp.int32, shape, dim)


def prep_kernel(kind, counts, known, tokens, cot, tokens_t, cot_t, packed, slot, meta):
    cells = known.shape[1] // SHORT_LENGTH if known.shape[0] == 1 else 4
    length = tokens.shape[0]
    is_long = kind[0] == 1
    row = iota(known.shape, 0)
    col = iota(known.shape, 1)
    limit = jnp.zeros(known.shape, jnp.int32)
    for cell in range(cells):
        limit = jnp.where(row == cell, counts[cell], limit)
    limit = jnp.where(is_long, counts[0] - SHORT_LENGTH * row, limit)
    first = (col == 0) & (jnp.logical_not(is_long) | (row == 0))
    usable = (col < limit) & ((known[...] == 1) | first) & (row < cells)
    usable_f = jnp.where(usable, 1.0, 0.0)
    square = (SHORT_LENGTH, SHORT_LENGTH)
    before = jnp.where(iota(square, 0) < iota(square, 1), 1.0, 0.0).astype(BF)
    rank = mm(usable_f.astype(BF), before, NN).astype(jnp.int32)
    totals = [jnp.sum(usable_f[cell : cell + 1, :]).astype(jnp.int32) for cell in range(cells)]
    base = jnp.zeros(known.shape, jnp.int32)
    running = jnp.int32(0)
    for cell in range(cells):
        start = jnp.where(is_long, running, SHORT_LENGTH * cell)
        base = jnp.where(row == cell, start, base)
        running = running + totals[cell]
    place = jnp.where(usable, rank + base, -1)
    for cell in range(cells):
        slot[0:1, pl.ds(cell * SHORT_LENGTH, SHORT_LENGTH)] = place[cell : cell + 1, :]
    meta[0] = kind[0]
    for cell in range(cells):
        meta[1 + cell] = jnp.where(is_long, running if cell == 0 else 0, totals[cell])

    for block in range(length // KEY_BLOCK):
        rows = pl.ds(block * KEY_BLOCK, KEY_BLOCK)
        tokens_t[:, rows] = tokens[rows, :].T
        cot_t[:, rows] = cot[rows, :].T
        cell = block * KEY_BLOCK // SHORT_LENGTH
        inside = block * KEY_BLOCK - cell * SHORT_LENGTH
        needed = jnp.where(is_long, block * KEY_BLOCK < running, inside < totals[cell])

        @pl.when(needed)
        def _(block=block, rows=rows):
            hot = one_hot(slot, block * KEY_BLOCK, KEY_BLOCK)
            packed[rows, :] = mm(hot, tokens[...], NN).astype(BF)


def one_hot(slot, begin, rows):
    shape = (rows, slot.shape[1])
    hit = (iota(shape, 0) + begin) == slot[0:1, :]
    return jnp.where(hit, 1.0, 0.0).astype(BF)


def prep(kind, counts, known, tokens, cot):
    length, width = tokens.shape
    cells = length // SHORT_LENGTH
    known = jnp.pad(known.reshape(cells, SHORT_LENGTH), ((0, 8 - cells), (0, 0)))
    return pl.pallas_call(
        prep_kernel,
        in_specs=[SMEM, SMEM, whole(8, SHORT_LENGTH), whole(length, width), whole(length, width)],
        out_specs=[
            whole(width, length),
            whole(width, length),
            whole(length, width),
            whole(1, length),
            SMEM,
        ],
        out_shape=[
            jax.ShapeDtypeStruct((width, length), BF),
            jax.ShapeDtypeStruct((width, length), BF),
            jax.ShapeDtypeStruct((length, width), BF),
            jax.ShapeDtypeStruct((1, length), jnp.int32),
            jax.ShapeDtypeStruct((8,), jnp.int32),
        ],
        compiler_params=params(),
        cost_estimate=cost(3e9, 12e6),
        name="prep",
    )(kind, counts, known, tokens, cot)


def fetch_rows(pieces, mine, target, sem):
    rows = pieces[0].shape[0]
    copies = []
    for index, piece in enumerate(pieces):
        owner = jnp.bitwise_xor(mine, index)
        place = target.at[pl.ds(pl.multiple_of(owner * rows, rows), rows), :]
        copies.append(pltpu.make_async_copy(piece, place, sem.at[index]))
    for copy in copies:
        copy.start()
    for copy in copies:
        copy.wait()


def head_lanes(shape, head):
    lane = iota(shape, 1)
    return (lane >= HDIM * head) & (lane < HDIM * (head + 1))


def spare(head):
    return HDIM * (1 - head)


def key_side(block, head, begin, count):
    lane = iota(block.shape, 1) - spare(head)
    row = iota(block.shape, 0) + begin
    bias = jnp.where(row < count, 0.0, MASKED)
    extra = jnp.where(lane == 0, bias, jnp.where((lane > 0) & (lane < 4), 1.0, 0.0))
    return jnp.where(head_lanes(block.shape, head), block.astype(F32), extra).astype(BF)


def value_side(block, head):
    lane = iota(block.shape, 1) - spare(head)
    extra = jnp.where((lane > 0) & (lane < 4), 1.0, 0.0)
    return jnp.where(head_lanes(block.shape, head), block.astype(F32), extra).astype(BF)


def split_rows(shift):
    high = shift.astype(BF).astype(F32)
    rest = shift - high
    mid = rest.astype(BF).astype(F32)
    low = rest - mid
    shape = (16, shift.shape[1])
    row = iota(shape, 0)
    out = jnp.where(row == 0, 1.0, 0.0)
    out = jnp.where(row == 1, -high, out)
    out = jnp.where(row == 2, -mid, out)
    return jnp.where(row == 3, -low, out).astype(BF)


def query_side(target, head, rows, shift):
    other = spare(head)
    target[head, HDIM * head : HDIM * (head + 1), :] = rows
    target[head, other : other + 16, :] = split_rows(shift)
    target[head, other + 16 : other + HDIM, :] = jnp.zeros((HDIM - 16, rows.shape[1]), BF)


def walk(meta, length, body):
    @pl.when(meta[0] == 1)
    def _():
        cell_walk(meta[1], 0, 0, length, body)

    @pl.when(meta[0] != 1)
    def _():
        for cell in range(length // SHORT_LENGTH):
            cell_walk(meta[1 + cell], cell * SHORT_LENGTH, cell * SHORT_LENGTH, SHORT_LENGTH, body)


def cell_walk(count, slot_begin, query_begin, queries, body):
    rest = lax.rem(count, KEY_BLOCK)
    tail = (rest > 0) & (rest <= TAIL)
    full = count // KEY_BLOCK + jnp.where(rest > TAIL, 1, 0)
    end = slot_begin + count

    @pl.loop(0, full)
    def _(index):
        begin = pl.multiple_of(slot_begin + index * KEY_BLOCK, KEY_BLOCK)
        body(begin, KEY_BLOCK, query_begin, queries, end)

    @pl.when(tail)
    def _():
        begin = pl.multiple_of(slot_begin + full * KEY_BLOCK, KEY_BLOCK)
        body(begin, TAIL, query_begin, queries, end)


def forward_kernel(count, mine, meta, *refs):
    pieces = refs[:count]
    tokens_t, packed, slot = refs[count : count + 3]
    q_out, k_out, v_out, kc_out, vc_out, kct_out, context, log_total = refs[count + 3 : count + 11]
    weights, vct, side, total, shift, sem = refs[count + 11 :]
    step = pl.program_id(0)
    length = tokens_t.shape[1]

    @pl.when(step == 0)
    def _():
        fetch_rows(pieces, mine[0], weights, sem)

    columns = pl.ds(pl.multiple_of(step * 3 * PAIR, 3 * PAIR), 3 * PAIR)
    part = weights[:, columns]
    joined = mm(part, tokens_t[...], TN)
    q_out[...] = (joined[:PAIR] * HDIM**-0.5).astype(BF)
    k_out[...] = joined[PAIR : 2 * PAIR].astype(BF)
    v_out[...] = joined[2 * PAIR :].astype(BF)

    def project(begin, rows, *_):
        place = pl.ds(begin, rows)
        both = mm(packed[place, :], part[:, PAIR:], NN).astype(BF)
        kc_out[place, :] = both[:, :PAIR]
        vc_out[place, :] = both[:, PAIR:]
        kct_out[:, place] = both[:, :PAIR].T
        turned = both[:, PAIR:].T
        ones = jnp.where(iota((16, rows), 0) == 0, 1.0, 0.0).astype(BF)
        for head in range(2):
            vct[head, :HDIM, place] = turned[HDIM * head : HDIM * (head + 1)]
            vct[head, HDIM:, place] = ones

    walk(meta, length, project)

    masked = slot[...] < 0
    own = []
    for head in range(2):
        rows = slice(HDIM * head, HDIM * (head + 1))
        queries = q_out[rows, :].astype(F32)
        keys = k_out[rows, :].astype(F32)
        own.append(jnp.where(masked, jnp.sum(queries * keys, axis=0, keepdims=True), MASKED))
        top_q = jnp.max(jnp.sum(queries * queries, axis=0, keepdims=True))
        top_k = jnp.max(jnp.sum(keys * keys, axis=0, keepdims=True))
        unsafe = jnp.logical_not(top_q * top_k < SAFE_SCORE * SAFE_SCORE)
        shift[head : head + 1, :] = jnp.zeros((1, length), F32)
        query_side(side, head, q_out[rows, :], jnp.zeros((1, length), F32))

        @pl.when(unsafe)
        def _(head=head, rows=rows):
            shift[head : head + 1, :] = own[head]

            def raise_top(begin, rows, first, queries, end):
                keys = key_side(kc_out[pl.ds(begin, rows), :], head, begin, end)
                place = pl.ds(first, queries)
                scores = mm(keys, side[head, :, place], NN)
                top = jnp.max(scores, axis=0, keepdims=True)
                shift[head : head + 1, place] = jnp.maximum(shift[head : head + 1, place], top)

            walk(meta, length, raise_top)
            query_side(side, head, q_out[rows, :], shift[head : head + 1, :])

    total[...] = jnp.zeros(total.shape, F32)

    def attend(begin, rows, first, queries, end):
        slots = pl.ds(begin, rows)
        place = pl.ds(first, queries)
        for head in range(2):
            keys = key_side(kc_out[slots, :], head, begin, end)
            raised = jnp.exp(mm(keys, side[head, :, place], NN)).astype(BF)
            total[head, :, place] += mm(vct[head, :, slots], raised, NN)

    walk(meta, length, attend)

    for head in range(2):
        rows = slice(HDIM * head, HDIM * (head + 1))
        alone = jnp.exp(own[head] - shift[head : head + 1, :])
        row_total = total[head, HDIM : HDIM + 1, :] + alone
        gathered = total[head, :HDIM, :] + v_out[rows, :].astype(F32) * alone
        context[rows, :] = (gathered / row_total).astype(BF)
        log_total[pl.ds(step * 2 + head, 1), :] = shift[head : head + 1, :] + jnp.log(row_total)


def forward(mine, meta, pieces, tokens_t, packed, slot):
    width, length = tokens_t.shape
    pair_rows = pl.BlockSpec((PAIR, length), lambda step: (step, 0))
    pair_lanes = pl.BlockSpec((length, PAIR), lambda step: (0, step))
    transposed = jax.ShapeDtypeStruct((width, length), BF)
    natural = jax.ShapeDtypeStruct((length, width), BF)
    count = len(pieces)
    return pl.pallas_call(
        partial(forward_kernel, count),
        grid=(PAIRS,),
        in_specs=[SMEM, SMEM]
        + [ANY] * count
        + [whole(width, length), whole(length, width), whole(1, length)],
        out_specs=[pair_rows] * 3 + [pair_lanes] * 2 + [pair_rows] * 2 + [whole(HEADS, length)],
        out_shape=[transposed] * 3
        + [natural] * 2
        + [transposed] * 2
        + [jax.ShapeDtypeStruct((HEADS, length), F32)],
        scratch_shapes=[
            pltpu.VMEM((width, 3 * width), BF),
            pltpu.VMEM((2, HDIM + 16, length), BF),
            pltpu.VMEM((2, PAIR, length), BF),
            pltpu.VMEM((2, HDIM + 16, length), F32),
            pltpu.VMEM((8, length), F32),
            pltpu.SemaphoreType.DMA((count,)),
        ],
        compiler_params=params(),
        cost_estimate=cost(15e9, 25e6, 20e6),
        name="attend_forward",
    )(mine, meta, *pieces, tokens_t, packed, slot)


def backward_kernel(pair, meta, *refs):
    q_t, k_t, v_t, kc, vc, kct, grad_context, log_total, inner, slot, tokens_t = refs[:11]
    grad_t, grad_weight = refs[11:13]
    q_side, g_side, grad_q, grad_kv, ready = refs[13:]
    length = tokens_t.shape[1]
    for head in range(2):
        rows = slice(HDIM * head, HDIM * (head + 1))
        index = 2 * pair + head
        query_side(q_side, head, q_t[rows, :], log_total[index : index + 1, :])
        query_side(g_side, head, grad_context[rows, :], inner[index : index + 1, :])
    grad_q[...] = jnp.zeros(grad_q.shape, F32)
    grad_kv[...] = jnp.zeros(grad_kv.shape, F32)

    def pull(begin, rows, first, queries, end):
        slots = pl.ds(begin, rows)
        place = pl.ds(first, queries)
        for head in range(2):
            lanes = slice(HDIM * head, HDIM * (head + 1))
            keys = key_side(kc[slots, :], head, begin, end)
            values = value_side(vc[slots, :], head)
            probs = jnp.exp(mm(keys, q_side[head, :, place], NN))
            grad_scores = (probs * mm(values, g_side[head, :, place], NN)).astype(BF)
            grad_q[lanes, place] += mm(kct[lanes, slots], grad_scores, NN)
            ready[HDIM * head : HDIM * (head + 1), :rows] = mm(
                q_t[lanes, place], grad_scores, NT
            ).astype(BF)
            ready[PAIR + HDIM * head : PAIR + HDIM * (head + 1), :rows] = mm(
                grad_context[lanes, place], probs.astype(BF), NT
            ).astype(BF)
        hit = (iota((rows, queries), 0) + begin) == slot[0:1, place]
        spread = jnp.where(hit, 1.0, 0.0).astype(BF)
        grad_kv[:, place] += mm(ready[:, :rows], spread, NN)

    walk(meta, length, pull)

    masked = slot[...] < 0
    for head in range(2):
        rows = slice(HDIM * head, HDIM * (head + 1))
        index = 2 * pair + head
        queries = q_t[rows, :].astype(F32)
        keys = k_t[rows, :].astype(F32)
        values = v_t[rows, :].astype(F32)
        grads = grad_context[rows, :].astype(F32)
        own = jnp.sum(queries * keys, axis=0, keepdims=True)
        own = jnp.where(masked, own - log_total[index : index + 1, :], MASKED)
        alone = jnp.exp(own)
        pulled = jnp.sum(grads * values, axis=0, keepdims=True) - inner[index : index + 1, :]
        pulled = (alone * pulled).astype(BF).astype(F32)
        alone = alone.astype(BF).astype(F32)
        part = (grad_q[rows, :] + keys * pulled) * HDIM**-0.5
        grad_t[HDIM * head : HDIM * (head + 1), :] = part.astype(BF)
        part = grad_kv[rows, :] + queries * pulled
        grad_t[PAIR + HDIM * head : PAIR + HDIM * (head + 1), :] = part.astype(BF)
        part = grad_kv[PAIR + HDIM * head : PAIR + HDIM * (head + 1), :] + grads * alone
        grad_t[2 * PAIR + HDIM * head : 2 * PAIR + HDIM * (head + 1), :] = part.astype(BF)
    grad_weight[...] = mm(tokens_t[...], grad_t[...], NT).astype(BF)


def backward(pair, meta, q_t, k_t, v_t, kc, vc, kct, grad_context, log_total, inner, slot, tokens_t):
    width, length = tokens_t.shape
    pair_rows = pl.BlockSpec((PAIR, length), lambda step: (pair, 0))
    pair_lanes = pl.BlockSpec((length, PAIR), lambda step: (0, pair))
    return pl.pallas_call(
        partial(backward_kernel, pair),
        grid=(1,),
        in_specs=[SMEM]
        + [pair_rows] * 3
        + [pair_lanes] * 2
        + [pair_rows] * 2
        + [whole(HEADS, length)] * 2
        + [whole(1, length), whole(width, length)],
        out_specs=[whole(3 * PAIR, length), whole(width, 3 * PAIR)],
        out_shape=[
            jax.ShapeDtypeStruct((3 * PAIR, length), BF),
            jax.ShapeDtypeStruct((width, 3 * PAIR), BF),
        ],
        scratch_shapes=[
            pltpu.VMEM((2, PAIR, length), BF),
            pltpu.VMEM((2, PAIR, length), BF),
            pltpu.VMEM((PAIR, length), F32),
            pltpu.VMEM((2 * PAIR, length), F32),
            pltpu.VMEM((2 * PAIR, KEY_BLOCK), BF),
        ],
        compiler_params=params(),
        cost_estimate=cost(12e9, 10e6, 6e6),
        name=f"attend_backward_{pair}",
    )(meta, q_t, k_t, v_t, kc, vc, kct, grad_context, log_total, inner, slot, tokens_t)


def feature_mean(values):
    return jnp.sum(values, axis=0, keepdims=True) * (1.0 / values.shape[0])


def normalise(values):
    centred = values - feature_mean(values)
    scale = lax.rsqrt(feature_mean(centred * centred) + NORM_EPS)
    return centred * scale, scale


def pull_norm(grad, scaled, scale, gain):
    lifted = grad * gain
    return scale * (lifted - feature_mean(lifted) - scaled * feature_mean(lifted * scaled))


def lane_sums(values):
    width = 128
    out = values[:, :width]
    for begin in range(width, values.shape[1], width):
        out = out + values[:, begin : begin + width]
    return out


def dense_kernel(count, mine, *refs):
    pieces = refs[:count]
    tokens_t, context, cot_t = refs[count : count + 3]
    out, grad_context, grad_first, inner, g_proj, g_up, g_down, g_norm = refs[count + 3 : count + 11]
    weights, total, norm_total, sem = refs[count + 11 :]
    step = pl.program_id(0)
    width = tokens_t.shape[0]

    @pl.when(step == 0)
    def _():
        fetch_rows(pieces, mine[0], weights, sem)
        total[...] = jnp.zeros(total.shape, F32)
        norm_total[...] = jnp.zeros(norm_total.shape, F32)

    proj = weights[:, :width]
    up = weights[:, width : 2 * width]
    down = weights[:, 2 * width : 3 * width]
    rows = weights[:, 3 * width :].astype(F32)
    gain1, bias1, gain2, bias2 = (rows[:, index : index + 1] for index in range(4))

    context_low = context[...]
    scaled1, scale1 = normalise(tokens_t[...].astype(F32) + mm(proj, context_low, TN))
    middle = scaled1 * gain1 + bias1
    middle_low = middle.astype(BF)
    hidden = mm(up, middle_low, TN)
    cdf = 0.5 * (1.0 + lax.erf(hidden * 2.0**-0.5))
    slope = cdf + hidden * jnp.exp(hidden * hidden * -0.5) * 0.3989422804014327
    active = (hidden * cdf).astype(BF)
    scaled2, scale2 = normalise(middle + mm(down, active, TN))
    out[...] = (scaled2 * gain2 + bias2).astype(BF).T

    cot = cot_t[...].astype(F32)
    norm_total[2] += lane_sums(cot * scaled2)
    norm_total[3] += lane_sums(cot)
    grad_second = pull_norm(cot, scaled2, scale2, gain2)
    grad_low = grad_second.astype(BF)
    total[2] += mm(active, grad_low, NT)
    grad_hidden = (mm(down, grad_low, NN) * slope).astype(BF)
    total[1] += mm(middle_low, grad_hidden, NT)
    grad_middle = grad_second + mm(up, grad_hidden, NN)
    norm_total[0] += lane_sums(grad_middle * scaled1)
    norm_total[1] += lane_sums(grad_middle)
    grad_h1 = pull_norm(grad_middle, scaled1, scale1, gain1)
    grad_first[...] = grad_h1
    proj_low = grad_h1.astype(BF)
    total[0] += mm(context_low, proj_low, NT)
    pulled = mm(proj, proj_low, NN).astype(BF)
    grad_context[...] = pulled
    both = pulled.astype(F32) * context_low.astype(F32)
    for head in range(HEADS):
        part = both[HDIM * head : HDIM * (head + 1), :]
        inner[head : head + 1, :] = jnp.sum(part, axis=0, keepdims=True)

    @pl.when(step == pl.num_programs(0) - 1)
    def _():
        g_proj[...] = total[0].astype(BF)
        g_up[...] = total[1].astype(BF)
        g_down[...] = total[2].astype(BF)
        lane = iota((width, 128), 1)
        packed = jnp.zeros((width, 128), F32)
        for index in range(4):
            column = jnp.sum(norm_total[index], axis=1, keepdims=True)
            packed = jnp.where(lane == index, column, packed)
        g_norm[...] = packed


def dense(mine, pieces, tokens_t, context, cot_t):
    width, length = tokens_t.shape
    block = 512
    count = len(pieces)
    columns = pl.BlockSpec((width, block), lambda step: (0, step))
    square = jax.ShapeDtypeStruct((width, width), BF)
    return pl.pallas_call(
        partial(dense_kernel, count),
        grid=(length // block,),
        in_specs=[SMEM] + [ANY] * count + [columns] * 3,
        out_specs=[
            pl.BlockSpec((block, width), lambda step: (step, 0)),
            columns,
            columns,
            pl.BlockSpec((HEADS, block), lambda step: (0, step)),
        ]
        + [whole(width, width)] * 3
        + [whole(width, 128)],
        out_shape=[
            jax.ShapeDtypeStruct((length, width), BF),
            jax.ShapeDtypeStruct((width, length), BF),
            jax.ShapeDtypeStruct((width, length), F32),
            jax.ShapeDtypeStruct((HEADS, length), F32),
        ]
        + [square] * 3
        + [jax.ShapeDtypeStruct((width, 128), F32)],
        scratch_shapes=[
            pltpu.VMEM((width, 3 * width + 128), BF),
            pltpu.VMEM((3, width, width), F32),
            pltpu.VMEM((4, width, 128), F32),
            pltpu.SemaphoreType.DMA((count,)),
        ],
        compiler_params=params(),
        cost_estimate=cost(10e9, 20e6, 4e6),
        name="dense",
    )(mine, *pieces, tokens_t, context, cot_t)


def input_kernel(count, mine, *refs):
    pieces = refs[:count]
    grads = refs[count : count + PAIRS]
    grad_first, out = refs[count + PAIRS : count + PAIRS + 2]
    weights, sem = refs[count + PAIRS + 2 :]

    @pl.when(pl.program_id(0) == 0)
    def _():
        fetch_rows(pieces, mine[0], weights, sem)

    total = grad_first[...]
    for pair in range(PAIRS):
        total = total + mm(weights[:, 3 * PAIR * pair : 3 * PAIR * (pair + 1)], grads[pair][...], NN)
    out[...] = total.astype(BF).T


def input_side(mine, pieces, grads, grad_first):
    width, length = grad_first.shape
    block = 512
    count = len(pieces)
    return pl.pallas_call(
        partial(input_kernel, count),
        grid=(length // block,),
        in_specs=[SMEM]
        + [ANY] * count
        + [pl.BlockSpec((3 * PAIR, block), lambda step: (0, step))] * PAIRS
        + [pl.BlockSpec((width, block), lambda step: (0, step))],
        out_specs=pl.BlockSpec((block, width), lambda step: (step, 0)),
        out_shape=jax.ShapeDtypeStruct((length, width), BF),
        scratch_shapes=[pltpu.VMEM((width, 3 * width), BF), pltpu.SemaphoreType.DMA((count,))],
        compiler_params=params(),
        cost_estimate=cost(3.3e9, 14e6),
        name="input_side",
    )(mine, *pieces, *grads, grad_first)


def swap(value, axis, size, mask):
    return lax.ppermute(value, axis, [(index, index ^ mask) for index in range(size)])


def masks_of(size):
    return [1 << bit for bit in range(size.bit_length() - 1)]


def gather_pieces(piece, axis, size):
    pieces = {0: piece}
    for mask in reversed(masks_of(size)):
        for known in list(pieces):
            pieces[known ^ mask] = swap(pieces[known], axis, size, mask)
    return [pieces[index] for index in range(size)]


def halve(value, axis, size, mask, index):
    keep = lax.dynamic_index_in_dim(value, index, 0, keepdims=False)
    send = lax.dynamic_index_in_dim(value, 1 - index, 0, keepdims=False)
    got = swap(send, axis, size, mask)
    return (keep.astype(F32) + got.astype(F32)).astype(BF)


def reduce_shard(grad, fsdp, dp):
    columns = grad.shape[1]
    mine = lax.axis_index("fsdp")
    rows = grad.shape[0] // fsdp
    value = grad.reshape(fsdp, rows, columns)
    for bit, mask in enumerate(masks_of(fsdp)):
        value = value.reshape(value.shape[0] // 2, 2, rows, columns).swapaxes(0, 1)
        value = halve(value, "fsdp", fsdp, mask, (mine >> bit) & 1)
    value = value.reshape(rows, columns)
    place = lax.axis_index("dp")
    taken = []
    for bit, mask in enumerate(masks_of(dp)):
        if value.shape[0] % 32:
            got = swap(value, "dp", dp, mask)
            value = (value.astype(F32) + got.astype(F32)).astype(BF)
            continue
        half = (place >> bit) & 1
        value = halve(value.reshape(2, -1, columns), "dp", dp, mask, half)
        taken.append((mask, half))
    for mask, half in reversed(taken):
        got = swap(value, "dp", dp, mask)
        first = jnp.where(half == 0, value, got)
        second = jnp.where(half == 0, got, value)
        value = jnp.concatenate([first, second], axis=0)
    return value.astype(F32)


def total_over(value, sizes):
    for axis, size in sizes:
        for mask in masks_of(size):
            value = value + swap(value, axis, size, mask)
    return value


def adam_terms(gradient, first_old, second_old):
    first_new = BETA * first_old + (1.0 - BETA) * gradient
    second_new = BETA * second_old + (1.0 - BETA) * gradient * gradient
    debias = 1.0 - BETA**STEP
    update = first_new / debias / (jnp.sqrt(second_new / debias) + ADAM_EPS)
    return (first_new, second_new, update)


def pair_major(columns):
    rows = columns.shape[0]
    return columns.reshape(rows, 3, PAIRS, PAIR).swapaxes(1, 2).reshape(rows, -1)


def shards(
    fsdp,
    dp,
    tokens,
    cotangent,
    known_genes,
    cell_kind,
    gene_counts,
    study_index,
    qkv_weight,
    qkv_first,
    qkv_second,
    proj_weight,
    proj_first,
    proj_second,
    up_weight,
    up_first,
    up_second,
    down_weight,
    down_first,
    down_second,
    norm_params,
    norm_first,
    norm_second,
):
    masters = (qkv_weight, proj_weight, up_weight, down_weight, norm_params)
    firsts_old = (qkv_first, proj_first, up_first, down_first, norm_first)
    seconds_old = (qkv_second, proj_second, up_second, down_second, norm_second)
    _, length, width = tokens.shape
    mine = lax.axis_index("fsdp").astype(jnp.int32)
    mine_ref = mine.reshape(1)
    sizes = (("fsdp", fsdp), ("dp", dp))

    qkv_pieces = gather_pieces(pair_major(qkv_weight.astype(BF)), "fsdp", fsdp)
    norm_columns = jnp.pad(norm_params.T, ((0, 0), (0, 124)))
    rest = jnp.concatenate([proj_weight, up_weight, down_weight, norm_columns], axis=1).astype(BF)
    rest, _ = lax.optimization_barrier((rest, qkv_pieces[-1]))
    rest_pieces = gather_pieces(rest, "fsdp", fsdp)

    tokens_t, cot_t, packed, slot, meta = prep(
        cell_kind, gene_counts.reshape(-1), known_genes.reshape(-1), tokens[0], cotangent[0]
    )
    q_t, k_t, v_t, kc, vc, kct, context, log_total = forward(
        mine_ref, meta, qkv_pieces, tokens_t, packed, slot
    )
    out, grad_context, grad_first, inner, g_proj, g_up, g_down, g_norm = dense(
        mine_ref, rest_pieces, tokens_t, context, cot_t
    )

    first_cells = out.reshape(-1, SHORT_LENGTH, width)[:, 0, :].astype(F32)
    slot_index = jnp.arange(first_cells.shape[0], dtype=jnp.int32)
    used_slots = (cell_kind[0] == 0) | (slot_index == 0)
    member = (
        (study_index[0][:, None] == jnp.arange(STUDY_COUNT, dtype=jnp.int32)[None, :])
        & used_slots[:, None]
    ).astype(F32)
    counts = jnp.broadcast_to(jnp.sum(member, axis=0)[:, None], (STUDY_COUNT, width))
    sums = jnp.sum(member[:, :, None] * first_cells[:, None, :], axis=0)
    squares = jnp.sum(member[:, :, None] * (first_cells * first_cells)[:, None, :], axis=0)
    small = jnp.concatenate([counts, sums, squares, g_norm[:, :8].T], axis=0)
    small = total_over(small, sizes)
    study_mean = small[8:16] / small[:8]
    study_var = small[16:24] / small[:8] - study_mean * study_mean
    norm_share = lax.dynamic_slice_in_dim(small[24:28], mine * (width // fsdp), width // fsdp, 1)

    side_share = reduce_shard(jnp.concatenate([g_proj, g_up, g_down], axis=1), fsdp, dp)
    grads = []
    weight_shares = []
    for pair in range(PAIRS):
        grad_t, grad_weight = backward(
            pair, meta, q_t, k_t, v_t, kc, vc, kct, grad_context, log_total, inner, slot, tokens_t
        )
        grads.append(grad_t)
        weight_shares.append(reduce_shard(grad_weight, fsdp, dp))
    input_grad = input_side(mine_ref, qkv_pieces, grads, grad_first)

    qkv_share = jnp.concatenate(
        [share[:, PAIR * kind : PAIR * (kind + 1)] for kind in range(3) for share in weight_shares],
        axis=1,
    )
    shares = (
        qkv_share,
        side_share[:, :width],
        side_share[:, width : 2 * width],
        side_share[:, 2 * width :],
        norm_share,
    )
    moved = [adam_terms(shares[index], firsts_old[index], seconds_old[index]) for index in range(5)]
    updates = [moved[index][2] + MATRIX_DECAY * masters[index] for index in range(4)]
    square_terms = [jnp.sum(masters[index] * masters[index]) for index in range(4)]
    square_terms = square_terms + [jnp.sum(updates[index] * updates[index]) for index in range(4)]
    total_squares = total_over(jnp.stack(square_terms), (("fsdp", fsdp),))
    weight_norms = jnp.sqrt(total_squares[:4])
    update_norms = jnp.sqrt(total_squares[4:])
    trust = weight_norms / update_norms
    results = []
    for index in range(5):
        if index < 4:
            new_weight = masters[index] - MATRIX_RATE * trust[index] * updates[index]
        else:
            new_weight = masters[index] - VECTOR_RATE * moved[index][2]
        results.extend(
            [moved[index][0], moved[index][1], new_weight, new_weight.astype(jnp.bfloat16)]
        )
    matrix_norms = jnp.stack([weight_norms, update_norms, trust])
    return (
        out.reshape(tokens.shape),
        input_grad.reshape(tokens.shape),
        study_mean,
        study_var,
        *results,
        matrix_norms,
    )


def solution(mesh):
    whole_groups = P(("dp", "fsdp"))
    rows = P("fsdp", None)
    columns = P(None, "fsdp")
    return jax.shard_map(
        partial(shards, mesh.shape["fsdp"], mesh.shape["dp"]),
        mesh=mesh,
        in_specs=(whole_groups,) * 6 + (rows,) * 12 + (columns,) * 3,
        out_specs=(whole_groups,) * 2 + (P(), P()) + (rows,) * 16 + (columns,) * 4 + (P(),),
        check_vma=False,
    )
```

time: 1120 us -> 324 us (0.29); the launches traced: 1100 us -> 326 us
  matrix products: 491 us -> 0 us
  other arithmetic: 229 us -> 17.4 us
  Pallas kernels: 0 us -> 164 us
  local copies, waits for them, and re-layouts: 131 us -> 14.5 us
  blocking collectives: 99.5 us -> 0 us
  starting transfers between devices: 0.29 us -> 76.2 us
  waiting for transfers between devices: 107 us -> 48.7 us
  loops' own time: 28.1 us -> 0 us
  between operations: 18.4 us -> 5.33 us
    dot_general x40 -> x0, matrix products: 491 us -> none  [the longest x8 166 us: masked_scores(): jnp.einsum('bhd,khd->hbk', query_block, keys, preferred_element_type=jnp....]
    pallas_call x0 -> x8, Pallas kernels: none -> 164 us  [the longest x4 71.8 us: backward(): pl.pallas_call(partial(backward_kernel, pair), grid=(1,), in_specs=[SMEM]...]
    convert_element_type x12 -> x32, other arithmetic: 119 us -> 4.8 us  [the longest x25 3.83 us: halve(): return (keep.astype(F32) + got.astype(F32)).astype(BF)]
    dynamic_update_slice x8 -> x0, local copies, waits for them, and re-layouts: 80.7 us -> none  [attend_forward(): context, log_total = lax.map(one_block, begins)]
    ppermute x0 -> x53, starting transfers between devices: none -> 76.2 us  [swap(): lax.ppermute(value, axis, [(index, index ^ mask) for index in range(size)])]
    reduce_sum x14 -> x2, other arithmetic: 73 us -> 0.17 us  [the longest x1 0.09 us: shards(): jnp.sum(member, axis=0)[:, None]]
    reduce_scatter x3 -> x0, waiting for transfers between devices: 67.6 us -> none  [the longest x1 24.2 us: shards(): lax.psum_scatter(local_grads[2].astype(jnp.bfloat16), 'fsdp', scatter_dim...]
    psum x3 -> x0, blocking collectives: 66.8 us -> none  [the longest x1 40 us: shards(): lax.psum((local_counts, local_sums, local_squares), ('dp', 'fsdp'))]
  transfers between devices with their start and end apart: 7 -> 53, of which waited for: 4 -> 18; matrix products, arithmetic and copies ran while one was open for 4% -> 4% of each run, Pallas kernels for 0% -> 20%
where the time goes in v1:
time: 324 us; the launch traced here: 326 us
  Pallas kernels  164 us (51%)
  starting transfers between devices  76.2 us (24%)
  waiting for transfers between devices  48.7 us (15%)
  other arithmetic  17.4 us (5%)
  local copies, waits for them, and re-layouts  14.5 us (4%)
  between operations  5.33 us (2%)
    ppermute x53, starting transfers between devices, swap(): lax.ppermute(value, axis, [(index, index ^ mask) for index in range(size)])  76.2 us
    pallas_call x4, Pallas kernels, backward(): pl.pallas_call(partial(backward_kernel, pair), grid=(1,), in_specs=[SMEM]...  71.8 us
    ppermute x53, waiting for transfers between devices, swap(): lax.ppermute(value, axis, [(index, index ^ mask) for index in range(size)])  48.7 us
    pallas_call x1, Pallas kernels, forward(): pl.pallas_call(partial(forward_kernel, count), grid=(PAIRS,), in_specs=[S...  46.7 us
    pallas_call x1, Pallas kernels, dense(): pl.pallas_call(partial(dense_kernel, count), grid=(length // block,), in_...  25.3 us
    pallas_call x1, Pallas kernels, input_side(): pl.pallas_call(partial(input_kernel, count), grid=(length // block,), in_...  10.2 us
    pallas_call x1, Pallas kernels, prep(): pl.pallas_call(prep_kernel, in_specs=[SMEM, SMEM, whole(8, SHORT_LENGTH),...  9.63 us
  transfers between devices with their start and end apart: 53, of which 18 were waited for; matrix products, arithmetic and copies ran while one was open for 4% of the time, Pallas kernels for 20%

profile of v1, /device:TPU:0, one launch (start us, length us, event | category | flops | bytes accessed | tf_op | source)
XLA Modules:
  0.0 325.9 jit_solution(7948574066100494295)
XLA Ops:
  2.4 3.0 collective-permute-start
  5.4 9.1 %collective-permute-done.refs_2_ = bf16[128,1536]{1,0:T(8,128)(2,1)S(1)} collective-permute-done((bf16[128,1536]{1,0:T(8,128)(2,1)S(1)}, bf16[128,1536]{1,0:T(8,128)(2,1)S(1)}, u32[]{:S(2)}, u32[]{:S(2)}) %collective-permute-start) | collective-permute-done | bytes 393248 | tf_op jit(solution)/shard_map/ppermute | solution.py:587
  20.0 9.6 %prep.1 = (bf16[512,2048]{1,0:T(8,128)(2,1)}, bf16[512,2048]{1,0:T(8,128)(2,1)}, bf16[2048,512]{1,0:T(8,128)(2,1)}, s32[1,2048]{1,0:T(1,128)}, s32[8]{0:T(128)}) custom-call(s32[1]{0:T(128)S(6)} %copy.124.kind, s32[4]{0:T(128)} %bitcast.217, s32[8,512]{1,0:T(8,128)} %pad.10.known, bf16[2048,512]{1,0:T(8,128)(2,1)} %bitcast.215, bf16[2048,512]{1,0:T(8,128)(2,1)} %bitcast.216), custom_call_target="tpu_custom_call" | custom-call | flops 3000000000 | bytes 12000000 | tf_op jit(solution)/shard_map/prep/pallas_call | solution.py:114
  31.0 46.7 %attend_forward.1 = (bf16[512,2048]{1,0:T(8,128)(2,1)}, bf16[512,2048]{1,0:T(8,128)(2,1)}, bf16[512,2048]{1,0:T(8,128)(2,1)}, bf16[2048,512]{1,0:T(8,128)(2,1)},...) custom-call(s32[1]{0:T(128)} %bitcast.mine, ...), custom_call_target="tpu_custom_call" | custom-call | flops 15000000512 | bytes 25000000 | tf_op jit(solution)/shard_map/attend_forward/pallas_call | solution.py:309
  78.8 25.3 %dense.1 = (bf16[2048,512]{1,0:T(8,128)(2,1)}, bf16[512,2048]{1,0:T(8,128)(2,1)}, f32[512,2048]{1,0:T(8,128)}, f32[8,2048]{1,0:T(8,128)}, bf16[512,512]{1,0:T(8,...) custom-call(s32[1]{0:T(128)} %bitcast.mine, bf16[128,1664]{1,0:T(8,128)(2,1)} %copy-done.16, ...), custom_call_target="tpu_custom_call" | custom-call | flops 10000000000 | bytes 20000000 | tf_op jit(solution)/shard_map/dense/pallas_call | solution.py:518
  105.7 17.8 %attend_backward_3.1 = (bf16[384,2048]{1,0:T(8,128)(2,1)}, bf16[512,384]{1,0:T(8,128)(2,1)}) custom-call(s32[8]{0:T(128)} %get-tuple-element.57.meta, bf16[512,2048]{1,0:T(8,128)(2,1)} %get-tuple-element.63.refs_0_, bf16[512,2048]{1,0:T(8,128)(2,1)} %get-tuple-element.64.refs_1_, bf16[512,2048]{1,0:T(8,128)(2,1)} %get-tuple-element.65.refs_2_, ...), custom_call_target="tpu_custom_call" | custom-call | flops 12000000000 | bytes 10000000 | tf_op jit(solution)/shard_map/attend_backward_3/pallas_call | solution.py:396
  123.5 17.9 %attend_backward_2.1 = (bf16[384,2048]{1,0:T(8,128)(2,1)}, bf16[512,384]{1,0:T(8,128)(2,1)}) custom-call(s32[8]{0:T(128)} %get-tuple-element.57.meta, bf16[512,2048]{1,0:T(8,128)(2,1)} %get-tuple-element.63.refs_0_, bf16[512,2048]{1,0:T(8,128)(2,1)} %get-tuple-element.64.refs_1_, bf16[512,2048]{1,0:T(8,128)(2,1)} %get-tuple-element.65.refs_2_, ...), custom_call_target="tpu_custom_call" | custom-call | flops 12000000000 | bytes 10000000 | tf_op jit(solution)/shard_map/attend_backward_2/pallas_call | solution.py:396
  141.4 18.1 %attend_backward_1.1 = (bf16[384,2048]{1,0:T(8,128)(2,1)}, bf16[512,384]{1,0:T(8,128)(2,1)}) custom-call(s32[8]{0:T(128)} %get-tuple-element.57.meta, bf16[512,2048]{1,0:T(8,128)(2,1)} %get-tuple-element.63.refs_0_, bf16[512,2048]{1,0:T(8,128)(2,1)} %get-tuple-element.64.refs_1_, bf16[512,2048]{1,0:T(8,128)(2,1)} %get-tuple-element.65.refs_2_, ...), custom_call_target="tpu_custom_call" | custom-call | flops 12000000000 | bytes 10000000 | tf_op jit(solution)/shard_map/attend_backward_1/pallas_call | solution.py:396
  159.6 18.0 %attend_backward_0.1 = (bf16[384,2048]{1,0:T(8,128)(2,1)}, bf16[512,384]{1,0:T(8,128)(2,1)}) custom-call(s32[8]{0:T(128)} %get-tuple-element.57.meta, bf16[512,2048]{1,0:T(8,128)(2,1)} %get-tuple-element.63.refs_0_, bf16[512,2048]{1,0:T(8,128)(2,1)} %get-tuple-element.64.refs_1_, bf16[512,2048]{1,0:T(8,128)(2,1)} %get-tuple-element.65.refs_2_, ...), custom_call_target="tpu_custom_call" | custom-call | flops 12000000000 | bytes 10000000 | tf_op jit(solution)/shard_map/attend_backward_0/pallas_call | solution.py:396
  182.1 10.2 %input_side.1 = bf16[2048,512]{1,0:T(8,128)(2,1)} custom-call(s32[1]{0:T(128)} %bitcast.mine, bf16[128,1536]{1,0:T(8,128)(2,1)} %copy-done.6, bf16[128,1536]{1,0:T(8,128)(2,1)} %copy-done.19, bf16[128,1536]{1,0:T(8,128)(2,1)} %copy-done.17, bf16[128,1536]{1,0:T(8,128)(2,1)} %copy-done.18, bf16[384,2048]{1,0:T(8,128)(2,1)} %get-tuple-element.72.refs_4_, ...), custom_call_target="tpu_custom_call" | custom-call | flops 3300000000 | bytes 14000000 | tf_op jit(solution)/shard_map/input_side/pallas_call | solution.py:570
  192.3 23.7 %collective-permute-start.8 = (f32[32,512]{1,0:T(8,128)S(1)}, f32[32,512]{1,0:T(8,128)S(1)}, u32[]{:S(2)}, u32[]{:S(2)}) collective-permute-start(f32[32,512]{1,0:T(8,128)S(1)} %add.252), channel_id=1, source_target_pairs={{0,4},{4,0},{8,12},{12,8},{16,20},{20,16},{24,28},{28,24},{1,5},{5... | collective-permute-start | bytes 196616 | tf_op jit(solution)/shard_map/ppermute | solution.py:587
  236.0 2.1 collective-permute-start.38
  238.3 2.1 collective-permute-start.14
  252.9 2.1 collective-permute-start.41
  267.0 6.7 %collective-permute-done.44 = bf16[1,128,1536]{2,1,0:T(8,128)(2,1)S(1)} collective-permute-done((bf16[1,128,1536]{2,1,0:T(8,128)(2,1)S(1)}, bf16[1,128,1536]{2,1,0:T(8,128)(2,1)S(1)}, u32[]{:S(2)}, u32[]{:S(2)}) %collective-permute-start.44) | collective-permute-done | bytes 393248 | tf_op jit(solution)/shard_map/ppermute | solution.py:587
  274.8 4.7 %collective-permute-done.45 = bf16[64,1536]{1,0:T(8,128)(2,1)S(1)} collective-permute-done((bf16[64,1536]{1,0:T(8,128)(2,1)S(1)}, bf16[64,1536]{1,0:T(8,128)(2,1)S(1)}, u32[]{:S(2)}, u32[]{:S(2)}) %collective-permute-start.45) | collective-permute-done | bytes 196640 | tf_op jit(solution)/shard_map/ppermute | solution.py:587
  281.2 3.1 collective-permute-done.46
  286.2 3.2 collective-permute-done.47
  291.2 3.2 collective-permute-done.48
  296.1 3.1 collective-permute-done.49
  302.0 3.0 collective-permute-done.50
  305.2 2.2 multiply_reduce_fusion.2
  307.4 5.3 %stack.47 = f32[8]{0:T(128)S(1)} concatenate(f32[1]{0:T(128)} %bitcast.62, f32[1]{0:T(128)} %bitcast.63, f32[1]{0:T(128)} %bitcast.64, f32[1]{0:T(128)} %bitcast.65, f32[1]{0:T(128)} %bitcast.66, f32[1]{0:T(128)} %bitcast.79, f32[1]{0:T(128)} %bitcast.80, f32[1]{0:T(128)} %bitcast.81), dimensions={0} | concatenate | bytes 64 | tf_op jit(solution)/shard_map/stack | solution.py:747
  314.8 2.5 collective-permute-done.52
  (306 shorter events, 77.8 us)
Async XLA Ops:
  2.4 12.1 %collective-permute-start = (bf16[128,1536]{1,0:T(8,128)(2,1)S(1)}, bf16[128,1536]{1,0:T(8,128)(2,1)S(1)}, u32[]{:S(2)}, u32[]{:S(2)}) collective-permute-start(bf16[128,1536]{1,0:T(8,128)(2,1)S(1)} %copy.104.refs_0_), channel_id=1, source_target_pairs={{0,2},{1,3},{2,0},{3,1},{4,6},{5,7},{6,4},{7,5},{8,10},{9,11},{10,... | collective-permute-start | bytes 1179656 | tf_op jit(solution)/shard_map/ppermute | solution.py:587
  14.5 15.7 %collective-permute-start.5 = (bf16[128,1536]{1,0:T(8,128)(2,1)S(1)}, bf16[128,1536]{1,0:T(8,128)(2,1)S(1)}, u32[]{:S(2)}, u32[]{:S(2)}) collective-permute-start(bf16[128,1536]{1,0:T(8,128)(2,1)S(1)} %copy.104.refs_0_), channel_id=1, source_target_pairs={{0,1},{1,0},{2,3},{3,2},{4,5},{5,4},{6,7},{7,6},{8,9},{9,8},{10,11... | collective-permute-start | bytes 1179656 | tf_op jit(solution)/shard_map/ppermute | solution.py:587
  16.3 13.5 %collective-permute-start.3 = (bf16[128,1664]{1,0:T(8,128)(2,1)S(1)}, bf16[128,1664]{1,0:T(8,128)(2,1)S(1)}, u32[]{:S(2)}, u32[]{:S(2)}) collective-permute-start(bf16[128,1664]{1,0:T(8,128)(2,1)S(1)} %fusion.3.refs_0_), channel_id=1, source_target_pairs={{0,2},{1,3},{2,0},{3,1},{4,6},{5,7},{6,4},{7,5},{8,10},{9,11},{10,... | collective-permute-start | bytes 1277960 | tf_op jit(solution)/shard_map/ppermute | solution.py:587
  29.7 48.1 %collective-permute-start.2 = (bf16[128,1664]{1,0:T(8,128)(2,1)S(1)}, bf16[128,1664]{1,0:T(8,128)(2,1)S(1)}, u32[]{:S(2)}, u32[]{:S(2)}) collective-permute-start(bf16[128,1664]{1,0:T(8,128)(2,1)S(1)} %fusion.3.refs_0_), channel_id=1, source_target_pairs={{0,1},{1,0},{2,3},{3,2},{4,5},{5,4},{6,7},{7,6},{8,9},{9,8},{10,11... | collective-permute-start | bytes 1277960 | tf_op jit(solution)/shard_map/ppermute | solution.py:587
  29.8 48.0 %collective-permute-start.4 = (bf16[128,1664]{1,0:T(8,128)(2,1)S(1)}, bf16[128,1664]{1,0:T(8,128)(2,1)S(1)}, u32[]{:S(2)}, u32[]{:S(2)}) collective-permute-start(bf16[128,1664]{1,0:T(8,128)(2,1)S(1)} %collective-permute-done.3.refs_2_), channel_id=1, source_target_pairs={{0,1},{1,0},{2,3},{3,2},{4,5},{5,4},{6,7},{7,6},{8,9},{9,8},{10,11... | collective-permute-start | bytes 1277960 | tf_op jit(solution)/shard_map/ppermute | solution.py:587
  178.1 87.5 %collective-permute-start.43 = (bf16[2,128,1536]{2,1,0:T(8,128)(2,1)S(1)}, bf16[2,128,1536]{2,1,0:T(8,128)(2,1)S(1)}, u32[]{:S(2)}, u32[]{:S(2)}) collective-permute-start(bf16[2,128,1536]{2,1,0:T(8,128)(2,1)S(1)} %dynamic-slice_bitcast_fusion), channel_id=1, source_target_pairs={{0,1},{1,0},{2,3},{3,2},{4,5},{5,4},{6,7},{7,6},{8,9},{9,8},{10,11... | collective-permute-start | bytes 2359304 | tf_op jit(solution)/shard_map/ppermute | solution.py:587
  179.6 39.1 %collective-permute-start.35 = (bf16[2,128,384]{2,1,0:T(8,128)(2,1)}, bf16[2,128,384]{2,1,0:T(8,128)(2,1)}, u32[]{:S(2)}, u32[]{:S(2)}) collective-permute-start(bf16[2,128,384]{2,1,0:T(8,128)(2,1)} %dynamic-slice_bitcast_fusion.2), channel_id=1, source_target_pairs={{0,1},{1,0},{2,3},{3,2},{4,5},{5,4},{6,7},{7,6},{8,9},{9,8},{10,11... | collective-permute-start | bytes 589832 | tf_op jit(solution)/shard_map/ppermute | solution.py:587
  180.7 39.2 %collective-permute-start.27 = (bf16[2,128,384]{2,1,0:T(8,128)(2,1)}, bf16[2,128,384]{2,1,0:T(8,128)(2,1)}, u32[]{:S(2)}, u32[]{:S(2)}) collective-permute-start(bf16[2,128,384]{2,1,0:T(8,128)(2,1)} %dynamic-slice_bitcast_fusion.3), channel_id=1, source_target_pairs={{0,1},{1,0},{2,3},{3,2},{4,5},{5,4},{6,7},{7,6},{8,9},{9,8},{10,11... | collective-permute-start | bytes 589832 | tf_op jit(solution)/shard_map/ppermute | solution.py:587
  181.5 41.3 %collective-permute-start.11 = (bf16[2,128,384]{2,1,0:T(8,128)(2,1)}, bf16[2,128,384]{2,1,0:T(8,128)(2,1)}, u32[]{:S(2)}, u32[]{:S(2)}) collective-permute-start(bf16[2,128,384]{2,1,0:T(8,128)(2,1)} %dynamic-slice_bitcast_fusion.5), channel_id=1, source_target_pairs={{0,1},{1,0},{2,3},{3,2},{4,5},{5,4},{6,7},{7,6},{8,9},{9,8},{10,11... | collective-permute-start | bytes 589832 | tf_op jit(solution)/shard_map/ppermute | solution.py:587
  182.0 10.2 %collective-permute-start.7 = (f32[32,512]{1,0:T(8,128)S(1)}, f32[32,512]{1,0:T(8,128)S(1)}, u32[]{:S(2)}, u32[]{:S(2)}) collective-permute-start(f32[32,512]{1,0:T(8,128)S(1)} %fusion.43), channel_id=1, source_target_pairs={{0,2},{1,3},{2,0},{3,1},{4,6},{5,7},{6,4},{7,5},{8,10},{9,11},{10,... | collective-permute-start | bytes 196616 | tf_op jit(solution)/shard_map/ppermute | solution.py:587
  192.3 26.4 %collective-permute-start.8 = (f32[32,512]{1,0:T(8,128)S(1)}, f32[32,512]{1,0:T(8,128)S(1)}, u32[]{:S(2)}, u32[]{:S(2)}) collective-permute-start(f32[32,512]{1,0:T(8,128)S(1)} %add.252), channel_id=1, source_target_pairs={{0,4},{4,0},{8,12},{12,8},{16,20},{20,16},{24,28},{28,24},{1,5},{5... | collective-permute-start | bytes 196616 | tf_op jit(solution)/shard_map/ppermute | solution.py:587
  218.7 7.4 %collective-permute-start.9 = (f32[32,512]{1,0:T(8,128)S(1)}, f32[32,512]{1,0:T(8,128)S(1)}, u32[]{:S(2)}, u32[]{:S(2)}) collective-permute-start(f32[32,512]{1,0:T(8,128)S(1)} %add.253), channel_id=1, source_target_pairs={{0,8},{4,12},{8,0},{12,4},{16,24},{20,28},{24,16},{28,20},{1,9},{5... | collective-permute-start | bytes 196616 | tf_op jit(solution)/shard_map/ppermute | solution.py:587
  219.9 6.6 %collective-permute-start.36 = (bf16[1,128,384]{2,1,0:T(8,128)(2,1)S(1)}, bf16[1,128,384]{2,1,0:T(8,128)(2,1)S(1)}, u32[]{:S(2)}, u32[]{:S(2)}) collective-permute-start(bf16[1,128,384]{2,1,0:T(8,128)(2,1)S(1)} %constant_dynamic-slice_fusion.4), channel_id=1, source_target_pairs={{0,2},{1,3},{2,0},{3,1},{4,6},{5,7},{6,4},{7,5},{8,10},{9,11},{10,... | collective-permute-start | bytes 294920 | tf_op jit(solution)/shard_map/ppermute | solution.py:587
  224.2 6.4 %collective-permute-start.12 = (bf16[1,128,384]{2,1,0:T(8,128)(2,1)S(1)}, bf16[1,128,384]{2,1,0:T(8,128)(2,1)S(1)}, u32[]{:S(2)}, u32[]{:S(2)}) collective-permute-start(bf16[1,128,384]{2,1,0:T(8,128)(2,1)S(1)} %constant_dynamic-slice_fusion.13), channel_id=1, source_target_pairs={{0,2},{1,3},{2,0},{3,1},{4,6},{5,7},{6,4},{7,5},{8,10},{9,11},{10,... | collective-permute-start | bytes 294920 | tf_op jit(solution)/shard_map/ppermute | solution.py:587
  226.1 6.4 %collective-permute-start.20 = (bf16[1,128,384]{2,1,0:T(8,128)(2,1)S(1)}, bf16[1,128,384]{2,1,0:T(8,128)(2,1)S(1)}, u32[]{:S(2)}, u32[]{:S(2)}) collective-permute-start(bf16[1,128,384]{2,1,0:T(8,128)(2,1)S(1)} %constant_dynamic-slice_fusion.10), channel_id=1, source_target_pairs={{0,2},{1,3},{2,0},{3,1},{4,6},{5,7},{6,4},{7,5},{8,10},{9,11},{10,... | collective-permute-start | bytes 294920 | tf_op jit(solution)/shard_map/ppermute | solution.py:587
  226.5 7.4 %collective-permute-start.10 = (f32[32,512]{1,0:T(8,128)S(1)}, f32[32,512]{1,0:T(8,128)S(1)}, u32[]{:S(2)}, u32[]{:S(2)}) collective-permute-start(f32[32,512]{1,0:T(8,128)S(1)} %add.254), channel_id=1, source_target_pairs={{0,16},{4,20},{8,24},{12,28},{16,0},{20,4},{24,8},{28,12},{1,17},{... | collective-permute-start | bytes 196616 | tf_op jit(solution)/shard_map/ppermute | solution.py:587
  228.5 7.5 %collective-permute-start.37 = (bf16[64,384]{1,0:T(8,128)(2,1)S(1)}, bf16[64,384]{1,0:T(8,128)(2,1)S(1)}, u32[]{:S(2)}, u32[]{:S(2)}) collective-permute-start(bf16[64,384]{1,0:T(8,128)(2,1)S(1)} %dynamic-slice_bitcast_fusion.8), channel_id=1, source_target_pairs={{0,4},{4,0},{8,12},{12,8},{16,20},{20,16},{24,28},{28,24},{1,5},{5... | collective-permute-start | bytes 147464 | tf_op jit(solution)/shard_map/ppermute | solution.py:587
  230.6 7.5 %collective-permute-start.29 = (bf16[64,384]{1,0:T(8,128)(2,1)S(1)}, bf16[64,384]{1,0:T(8,128)(2,1)S(1)}, u32[]{:S(2)}, u32[]{:S(2)}) collective-permute-start(bf16[64,384]{1,0:T(8,128)(2,1)S(1)} %dynamic-slice_bitcast_fusion.9), channel_id=1, source_target_pairs={{0,4},{4,0},{8,12},{12,8},{16,20},{20,16},{24,28},{28,24},{1,5},{5... | collective-permute-start | bytes 147464 | tf_op jit(solution)/shard_map/ppermute | solution.py:587
  233.9 6.5 %collective-permute-start.21 = (bf16[64,384]{1,0:T(8,128)(2,1)S(1)}, bf16[64,384]{1,0:T(8,128)(2,1)S(1)}, u32[]{:S(2)}, u32[]{:S(2)}) collective-permute-start(bf16[64,384]{1,0:T(8,128)(2,1)S(1)} %dynamic-slice_bitcast_fusion.10), channel_id=1, source_target_pairs={{0,4},{4,0},{8,12},{12,8},{16,20},{20,16},{24,28},{28,24},{1,5},{5... | collective-permute-start | bytes 147464 | tf_op jit(solution)/shard_map/ppermute | solution.py:587
  240.5 6.2 %collective-permute-start.39 = (bf16[16,384]{1,0:T(8,128)(2,1)S(1)}, bf16[16,384]{1,0:T(8,128)(2,1)S(1)}, u32[]{:S(2)}, u32[]{:S(2)}) collective-permute-start(bf16[16,384]{1,0:T(8,128)(2,1)S(1)} %fusion.34), channel_id=1, source_target_pairs={{0,16},{4,20},{8,24},{12,28},{16,0},{20,4},{24,8},{28,12},{1,17},{... | collective-permute-start | bytes 36872 | tf_op jit(solution)/shard_map/ppermute | solution.py:587
  248.3 6.7 %collective-permute-start.32 = (bf16[16,384]{1,0:T(8,128)(2,1)S(1)}, bf16[16,384]{1,0:T(8,128)(2,1)S(1)}, u32[]{:S(2)}, u32[]{:S(2)}) collective-permute-start(bf16[16,384]{1,0:T(8,128)(2,1)S(1)} %fusion.23), channel_id=1, source_target_pairs={{0,16},{4,20},{8,24},{12,28},{16,0},{20,4},{24,8},{28,12},{1,17},{... | collective-permute-start | bytes 36872 | tf_op jit(solution)/shard_map/ppermute | solution.py:587
  257.4 8.0 %collective-permute-start.42 = (bf16[64,384]{1,0:T(8,128)(2,1)S(1)}, bf16[64,384]{1,0:T(8,128)(2,1)S(1)}, u32[]{:S(2)}, u32[]{:S(2)}) collective-permute-start(bf16[64,384]{1,0:T(8,128)(2,1)S(1)} %pad_maximum_fusion.7), channel_id=1, source_target_pairs={{0,4},{4,0},{8,12},{12,8},{16,20},{20,16},{24,28},{28,24},{1,5},{5... | collective-permute-start | bytes 147464 | tf_op jit(solution)/shard_map/ppermute | solution.py:587
  258.9 6.5 %collective-permute-start.34 = (bf16[64,384]{1,0:T(8,128)(2,1)S(1)}, bf16[64,384]{1,0:T(8,128)(2,1)S(1)}, u32[]{:S(2)}, u32[]{:S(2)}) collective-permute-start(bf16[64,384]{1,0:T(8,128)(2,1)S(1)} %pad_maximum_fusion.6), channel_id=1, source_target_pairs={{0,4},{4,0},{8,12},{12,8},{16,20},{20,16},{24,28},{28,24},{1,5},{5... | collective-permute-start | bytes 147464 | tf_op jit(solution)/shard_map/ppermute | solution.py:587
  265.8 7.8 %collective-permute-start.44 = (bf16[1,128,1536]{2,1,0:T(8,128)(2,1)S(1)}, bf16[1,128,1536]{2,1,0:T(8,128)(2,1)S(1)}, u32[]{:S(2)}, u32[]{:S(2)}) collective-permute-start(bf16[1,128,1536]{2,1,0:T(8,128)(2,1)S(1)} %constant_dynamic-slice_fusion.1), channel_id=1, source_target_pairs={{0,2},{1,3},{2,0},{3,1},{4,6},{5,7},{6,4},{7,5},{8,10},{9,11},{10,... | collective-permute-start | bytes 1179656 | tf_op jit(solution)/shard_map/ppermute | solution.py:587
  (69 other events, 715.2 us)
